TPU v7x, 512 devices: a whole 4x8x8 slice. The times are simulated.
512 devices in a mesh: pb: 32 (over z_hi, y, core), ka: 16 (over x, z_lo).
Axes of the slice: x: 4, y: 8, z: 8 (z_hi: 2, z_lo: 4; z = z_hi * 4 + z_lo), core: 2. Of those that a mesh axis runs over, the one named last changes fastest.
Arguments:
- single_track: bfloat16 [2048, 384], P('pb'), may hold values from -48 to 48
- pair_track: bfloat16 [2048, 2048, 128], P('pb', 'ka'), may hold values from -80 to 80
- token_mask: int32 [2048], P('ka'), may hold values 0 or 1
- out_cotangent: bfloat16 [2048, 384], P('pb'), may hold values from -6 to 6
- query_weight: bfloat16 [384, 384], P('ka'), may hold values from -0.3125 to 0.3125
- query_bias: bfloat16 [384], replicated, may hold values from -4 to 4
- key_weight: bfloat16 [384, 384], P('ka'), may hold values from -0.3125 to 0.3125
- value_weight: bfloat16 [384, 384], P('ka'), may hold values from -0.3125 to 0.3125
- gate_weight: bfloat16 [384, 384], P('ka'), may hold values from -0.3125 to 0.3125
- output_weight: bfloat16 [384, 384], P('ka'), may hold values from -0.3125 to 0.3125
- pair_weight: bfloat16 [128, 16], replicated, may hold values from -1.5 to 30.125
Outputs:
- attention_out: bfloat16 [2048, 384], P('pb')
- single_grad: bfloat16 [2048, 384], P('pb')
- pair_grad: bfloat16 [2048, 2048, 128], P('pb', 'ka')
Inputs may be any that keep to these rules, and one draw needn't show every extreme that they name: `token_mask`: 1 marks a real token, 0 padding.
All inputs are finite; a program needn't handle non-finite values. No bound on the sum of `token_mask` on one device may be relied on, other than what follows from the above.
Results may differ from a plain program's by a relative error of at most 0.0103.
Values may be sent and summed in bfloat16 or wider, within the bound.
A program may use at most 64 MiB of HBM per device.

v0:
```python
import jax
import jax.numpy as jnp
from jax import lax
from jax.sharding import PartitionSpec as P

NORM_EPSILON = 1e-05
MASK_PENALTY = 1000000000.0
WIDE_TYPE = jnp.float32
NARROW_TYPE = jnp.bfloat16
HIGHEST = lax.Precision.HIGHEST


def normalize(values):
    widened = values.astype(WIDE_TYPE)
    centred = widened - jnp.mean(widened, axis=-1, keepdims=True)
    inverse = lax.rsqrt(jnp.mean(centred * centred, axis=-1, keepdims=True) + NORM_EPSILON)
    return (centred * inverse, inverse)


def norm_back(gradient, normed, inverse):
    return inverse * (
        gradient
        - jnp.mean(gradient, axis=-1, keepdims=True)
        - normed * jnp.mean(gradient * normed, axis=-1, keepdims=True)
    )


def exact_product(first_operand, weight_matrix):
    return jnp.dot(first_operand, weight_matrix.astype(WIDE_TYPE), precision=HIGHEST)


def local(
    single_track,
    pair_track,
    token_mask,
    out_cotangent,
    query_weight,
    query_bias,
    key_weight,
    value_weight,
    gate_weight,
    output_weight,
    pair_weight,
):
    query_weight, key_weight, value_weight, gate_weight, output_weight = (
        lax.all_gather(query_weight, "ka", axis=0, tiled=True),
        lax.all_gather(key_weight, "ka", axis=0, tiled=True),
        lax.all_gather(value_weight, "ka", axis=0, tiled=True),
        lax.all_gather(gate_weight, "ka", axis=0, tiled=True),
        lax.all_gather(output_weight, "ka", axis=0, tiled=True),
    )
    row_count, feature_count = single_track.shape
    key_count = pair_track.shape[1]
    head_count = pair_weight.shape[1]
    head_dim = feature_count // head_count
    score_scale = head_dim ** (-0.5)
    owner_count = lax.axis_size("pb") // lax.axis_size("ka")
    query_index = lax.axis_index("pb")
    key_index = lax.axis_index("ka")
    normed_single, single_inverse = normalize(single_track)
    attention_input = normed_single.astype(NARROW_TYPE)
    query_rows = (
        jnp.dot(attention_input, query_weight, preferred_element_type=WIDE_TYPE)
        + query_bias.astype(WIDE_TYPE)
    ).astype(NARROW_TYPE)
    gate_value = jax.nn.sigmoid(
        jnp.dot(attention_input, gate_weight, preferred_element_type=WIDE_TYPE)
    )
    joint_weight = jnp.concatenate([key_weight, value_weight], axis=1)
    local_joint = jnp.dot(attention_input, joint_weight, preferred_element_type=WIDE_TYPE).astype(
        NARROW_TYPE
    )
    all_joint = lax.all_gather(local_joint, "pb", axis=0, tiled=True)
    joint_rows = lax.dynamic_slice_in_dim(all_joint, key_index * key_count, key_count, 0)
    key_heads = joint_rows[:, :feature_count].reshape(key_count, head_count, head_dim)
    value_heads = joint_rows[:, feature_count:].reshape(key_count, head_count, head_dim)
    query_heads = query_rows.reshape(row_count, head_count, head_dim)
    pair_normed, pair_inverse = normalize(pair_track)
    weight_bias = pair_weight.astype(WIDE_TYPE)
    pair_bias = jnp.einsum("ijc,ch->hij", pair_normed, weight_bias, precision=HIGHEST)
    penalty = (token_mask.astype(WIDE_TYPE) - 1.0) * MASK_PENALTY
    logits = (
        jnp.einsum("ihd,jhd->hij", query_heads, key_heads, preferred_element_type=WIDE_TYPE)
        * score_scale
        + pair_bias
        + penalty
    )
    row_max = lax.pmax(jnp.max(logits, axis=-1), "ka")
    exp_scores = jnp.exp(logits - row_max[:, :, None])
    local_numerator = jnp.einsum(
        "hij,jhd->ihd",
        exp_scores.astype(NARROW_TYPE),
        value_heads,
        preferred_element_type=WIDE_TYPE,
    )
    totals, numerator = lax.psum(
        (jnp.sum(exp_scores, axis=-1), local_numerator.reshape(row_count, feature_count)), "ka"
    )
    attended = numerator.reshape(row_count, head_count, head_dim) / totals.T[:, :, None]
    attended_flat = attended.reshape(row_count, feature_count)
    gated_values = (gate_value * attended_flat).astype(NARROW_TYPE)
    attention_out = jnp.dot(gated_values, output_weight, preferred_element_type=WIDE_TYPE).astype(
        NARROW_TYPE
    )
    cotangent_rows = jnp.dot(out_cotangent, output_weight.T, preferred_element_type=WIDE_TYPE)
    attended_grad = (gate_value * cotangent_rows).astype(NARROW_TYPE)
    gate_input_grad = cotangent_rows * attended_flat * gate_value * (1.0 - gate_value)
    grad_heads = attended_grad.reshape(row_count, head_count, head_dim)
    row_delta = jnp.sum(grad_heads.astype(WIDE_TYPE) * attended, axis=-1)
    softmax_rows = exp_scores / totals[:, :, None]
    prob_grads = jnp.einsum(
        "ihd,jhd->hij", grad_heads, value_heads, preferred_element_type=WIDE_TYPE
    )
    score_grad = softmax_rows * (prob_grads - row_delta.T[:, :, None])
    score_weights = score_grad.astype(NARROW_TYPE)
    query_grad = (
        jnp.einsum("hij,jhd->ihd", score_weights, key_heads, preferred_element_type=WIDE_TYPE)
        * score_scale
    ).reshape(row_count, feature_count)
    key_grad = (
        jnp.einsum("hij,ihd->jhd", score_weights, query_heads, preferred_element_type=WIDE_TYPE)
        * score_scale
    ).reshape(key_count, feature_count)
    value_grad = jnp.einsum(
        "hij,ihd->jhd",
        softmax_rows.astype(NARROW_TYPE),
        grad_heads,
        preferred_element_type=WIDE_TYPE,
    ).reshape(key_count, feature_count)
    channel_grad = jnp.einsum("hij,ch->ijc", score_grad, weight_bias, precision=HIGHEST)
    pair_grad = norm_back(channel_grad, pair_normed, pair_inverse).astype(NARROW_TYPE)
    summed_keys, summed_values = lax.psum((key_grad, value_grad), "pb")
    key_input = exact_product(summed_keys, key_weight.T) + exact_product(
        summed_values, value_weight.T
    )
    owned_rows = lax.dynamic_slice_in_dim(
        key_input, query_index % owner_count * row_count, row_count, 0
    )
    is_owner = key_index == query_index // owner_count
    row_terms = exact_product(query_grad, query_weight.T) + jnp.where(is_owner, owned_rows, 0.0)
    input_grad = lax.psum(row_terms, "ka") + exact_product(gate_input_grad, gate_weight.T)
    single_grad = norm_back(input_grad, normed_single, single_inverse).astype(NARROW_TYPE)
    return (attention_out, single_grad, pair_grad)


def solution(mesh):
    in_specs = (
        P("pb", None),
        P("pb", "ka", None),
        P("ka"),
        P("pb", None),
        P("ka", None),
        P(),
        P("ka", None),
        P("ka", None),
        P("ka", None),
        P("ka", None),
        P(),
    )
    out_specs = (P("pb", None), P("pb", None), P("pb", "ka", None))
    return jax.shard_map(local, mesh=mesh, in_specs=in_specs, out_specs=out_specs, check_vma=False)
```

profile of v0, /device:TPU:56, one launch (start us, length us, event | category | flops | bytes accessed | tf_op | source)
XLA Modules:
  0.0 999.8 jit_solution(5748669555895392937)
XLA Ops:
  7.2 0.0 copy-start
  7.2 0.0 all-gather.2.cloned.1.call-start
  7.2 0.9 convert_reduce_fusion.1
  8.2 1.0 fusion.45
  9.2 0.0 copy-start.19
  9.2 48.0 %all_gather.19 = bf16[384,384]{1,0:T(8,128)(2,1)S(1)} all-gather(bf16[24,384]{1,0:T(8,128)(2,1)} %param.17), channel_id=1, replica_groups=mesh['pb'=32,'ka'=16] {'ka'}, dimensions={0}, use_global_device_ids=true | all-gather | bytes 313344 | tf_op jit(solution)/shard_map/all_gather | solution.py:47
  57.2 39.6 %all_gather.20 = bf16[384,384]{1,0:T(8,128)(2,1)S(1)} all-gather(bf16[24,384]{1,0:T(8,128)(2,1)} %param.18), channel_id=1, replica_groups=mesh['pb'=32,'ka'=16] {'ka'}, dimensions={0}, use_global_device_ids=true | all-gather | bytes 313344 | tf_op jit(solution)/shard_map/all_gather | solution.py:48
  96.7 1.7 convolution_convert_fusion
  98.5 0.0 all-gather.2.cloned.1.call-update
  98.5 0.0 all-reduce.5.cloned.1.call-start
  98.6 0.7 convert_element_type.56
  99.3 41.4 %all_gather.22 = bf16[384,384]{1,0:T(8,128)(2,1)S(1)} all-gather(bf16[24,384]{1,0:T(8,128)(2,1)} %param.15), channel_id=1, replica_groups=mesh['pb'=32,'ka'=16] {'ka'}, dimensions={0}, use_global_device_ids=true | all-gather | bytes 313344 | tf_op jit(solution)/shard_map/all_gather | solution.py:46
  140.7 1.0 fusion.19
  141.7 0.0 copy-start.23
  141.7 0.7 copy.30
  142.5 44.9 %all_gather.18 = bf16[384,384]{1,0:T(8,128)(2,1)S(1)} all-gather(bf16[24,384]{1,0:T(8,128)(2,1)} %param.19), channel_id=1, replica_groups=mesh['pb'=32,'ka'=16] {'ka'}, dimensions={0}, use_global_device_ids=true | all-gather | bytes 313344 | tf_op jit(solution)/shard_map/all_gather | solution.py:49
  187.4 41.9 %all_gather.23 = bf16[384,384]{1,0:T(8,128)(2,1)S(1)} all-gather(bf16[24,384]{1,0:T(8,128)(2,1)} %param.20), channel_id=1, replica_groups=mesh['pb'=32,'ka'=16] {'ka'}, dimensions={0}, use_global_device_ids=true | all-gather | bytes 313344 | tf_op jit(solution)/shard_map/all_gather | solution.py:50
  229.3 0.2 fusion.64
  229.5 0.6 copy-done.11
  230.2 1.7 multiply_convert_fusion
  231.8 0.7 copy.37
  232.6 3.2 copy.32
  235.8 0.5 convert_reduce_fusion
  236.4 0.5 add_multiply_fusion
  236.9 0.8 fusion.10
  237.7 0.0 copy-start.14
  237.7 0.6 copy-done.14
  238.3 0.0 copy-done.21
  238.3 2.6 fusion.4
  241.0 1.0 constant_dynamic-slice_fusion
  241.9 0.7 copy.31
  242.7 0.7 copy.29
  243.4 2.2 fusion.63
  245.6 39.3 %pmax.7 = f32[16,64]{1,0:T(8,128)} all-reduce(f32[16,64]{1,0:T(8,128)} %get-tuple-element.17), channel_id=1, replica_groups=mesh['pb'=32,'ka'=16] {'ka'}, use_global_device_ids=true, to_apply=%region_5.0 | all-reduce | flops 1024 | bytes 8192 | tf_op jit(solution)/shard_map/pmax | solution.py:88
  284.9 1.7 fusion.26
  286.6 41.4 %psum.36 = f32[16,64]{1,0:T(8,128)} all-reduce(f32[16,64]{1,0:T(8,128)} %fusion.26), channel_id=1, replica_groups=mesh['pb'=32,'ka'=16] {'ka'}, use_global_device_ids=true, to_apply=%region_8.0 | all-reduce | flops 1024 | bytes 8192 | tf_op jit(solution)/shard_map/psum | solution.py:96
  328.0 1.9 fusion.28
  329.9 1.7 copy.35
  331.6 0.0 all-reduce.5.cloned.1.call-update
  331.6 0.0 all-reduce.9.cloned.1.call-start
  331.6 2.0 fusion.30
  333.7 1.4 div.61
  335.1 1.7 copy.36
  336.7 151.9 %all-reduce.5.cloned.1.call-done = f32[64,384]{1,0:T(8,128)} async-done(((f32[64,384]{1,0:T(8,128)}), f32[64,384]{1,0:T(8,128)}) %all-reduce.5.cloned.1.call-update) | async-done | bytes 98320 | tf_op jit(solution)/shard_map/psum | solution.py:96
  488.6 1.7 copy.38
  490.4 1.0 multiply_reduce_fusion
  491.4 1.6 fusion.15
  492.9 1.8 convolution_multiply_fusion.1
  494.7 1.8 convolution_multiply_fusion.2
  496.6 0.0 copy-done.9
  496.6 4.6 fusion.61
  501.2 0.0 all-reduce.9.cloned.1.call-update
  501.2 0.2 all-reduce.7.cloned.1.call-start
  501.5 4.9 fusion.9
  506.4 323.5 %all-reduce.9.cloned.1.call-done = (f32[128,384]{0,1:T(8,128)}, f32[128,384]{0,1:T(8,128)}) async-done(((f32[128,384]{0,1:T(8,128)}, f32[128,384]{0,1:T(8,128)}), (f32[128,384]{0,1:T(8,128)}, f32[128,384]{0,1:T(8,128)})) %all-reduce.9.cloned.1.call-update) | async-done | bytes 393232 | tf_op jit(solution)/shard_map/psum | solution.py:132
  829.9 1.6 fusion.65
  831.5 1.4 fusion.66
  832.9 2.1 convolution_add_fusion.1
  835.1 0.0 all-reduce.7.cloned.1.call-update
  835.1 1.7 convolution_convert_fusion.1
  836.8 2.9 copy.40
  839.7 151.3 %all-reduce.7.cloned.1.call-done = f32[64,384]{1,0:T(8,128)} async-done(((f32[64,384]{1,0:T(8,128)}), f32[64,384]{1,0:T(8,128)}) %all-reduce.7.cloned.1.call-update) | async-done | bytes 98320 | tf_op jit(solution)/shard_map/psum | solution.py:141
  991.1 1.4 fusion.62
  992.5 0.7 fusion.44
  (47 shorter events, 0.1 us)
Async XLA Ops:
  7.2 222.1 %copy-start = (bf16[64,384]{1,0:T(8,128)(2,1)S(1)}, bf16[64,384]{1,0:T(8,128)(2,1)}, u32[]{:S(2)}) copy-start(bf16[64,384]{1,0:T(8,128)(2,1)} %param.14) | copy-start | bytes 147460
  7.2 233.8 %all-gather.2.cloned.1.call-start = ((), (), s32[]{:S(2)}) async-start(), calls=%async_computation | async-start | bytes 3244032 | tf_op jit(solution)/shard_map/all_gather | solution.py:73
  8.1 223.7 %copy-start.17 = (f32[64]{0:T(128)}, f32[64]{0:T(128)S(1)}, u32[]{:S(2)}) copy-start(f32[64]{0:T(128)S(1)} %broadcast_multiply_fusion.5) | copy-start | bytes 772
  9.2 222.7 %copy-start.19 = (f32[64]{0:T(128)}, f32[64]{0:T(128)S(1)}, u32[]{:S(2)}) copy-start(f32[64]{0:T(128)S(1)} %add_rsqrt_fusion.1) | copy-start | bytes 772
  57.2 84.5 %copy-start.5 = (bf16[384,384]{1,0:T(8,128)(2,1)}, bf16[384,384]{1,0:T(8,128)(2,1)S(1)}, u32[]{:S(2)}) copy-start(bf16[384,384]{1,0:T(8,128)(2,1)S(1)} %all_gather.19) | copy-start | bytes 884740
  96.7 45.7 %copy-start.3 = (bf16[384,384]{1,0:T(8,128)(2,1)}, bf16[384,384]{1,0:T(8,128)(2,1)S(1)}, u32[]{:S(2)}) copy-start(bf16[384,384]{1,0:T(8,128)(2,1)S(1)} %all_gather.20) | copy-start | bytes 884740
  98.5 390.1 %all-reduce.5.cloned.1.call-start = ((), (), s32[]{:S(2)}) async-start(), calls=%async_computation.1 | async-start | bytes 196608 | tf_op jit(solution)/shard_map/psum | solution.py:96
  141.7 94.6 %copy-start.23 = (s32[128]{0:T(128)S(1)}, s32[128]{0:T(128)}, u32[]{:S(2)}) copy-start(s32[128]{0:T(128)} %param.13) | copy-start | bytes 1540
  229.5 0.6 copy-start.11
  232.6 5.8 copy-start.21
  236.9 0.8 copy-start.8
  237.7 0.6 copy-start.14
  331.6 498.3 %all-reduce.9.cloned.1.call-start = ((), (), s32[]{:S(2)}) async-start(), calls=%async_computation.3 | async-start | bytes 786432 | tf_op jit(solution)/shard_map/psum | solution.py:132
  490.3 6.2 copy-start.9
  490.3 6.2 copy-start.15
  490.3 6.2 copy-start.22
  494.7 6.7 copy-start.10
  494.7 6.8 copy-start.16
  501.2 489.8 %all-reduce.7.cloned.1.call-start = ((), (), s32[]{:S(2)}) async-start(), calls=%async_computation.2 | async-start | bytes 196608 | tf_op jit(solution)/shard_map/psum | solution.py:141
  501.5 330.0 %copy-start.4 = (bf16[384,384]{1,0:T(8,128)(2,1)S(1)}, bf16[384,384]{1,0:T(8,128)(2,1)}, u32[]{:S(2)}) copy-start(bf16[384,384]{1,0:T(8,128)(2,1)} %copy-done.3) | copy-start | bytes 884740
  501.5 333.6 %copy-start.6 = (f32[64,384]{1,0:T(8,128)S(1)}, f32[64,384]{1,0:T(8,128)}, u32[]{:S(2)}) copy-start(f32[64,384]{1,0:T(8,128)} %all-reduce.5.cloned.1.call-done) | copy-start | bytes 294916
  506.4 330.4 %copy-start.1 = (bf16[64,128,128]{1,2,0:T(8,128)(2,1)S(1)}, bf16[64,128,128]{1,2,0:T(8,128)(2,1)}, u32[]{:S(2)}) copy-start(bf16[64,128,128]{1,2,0:T(8,128)(2,1)} %fusion.9) | copy-start | bytes 6291460
  506.4 484.6 %copy-start.2 = (bf16[64,384]{1,0:T(8,128)(2,1)S(1)}, bf16[64,384]{1,0:T(8,128)(2,1)}, u32[]{:S(2)}) copy-start(bf16[64,384]{1,0:T(8,128)(2,1)} %param.11) | copy-start | bytes 147460
  506.4 484.6 %copy-start.18 = (f32[64]{0:T(128)S(1)}, f32[64]{0:T(128)}, u32[]{:S(2)}) copy-start(f32[64]{0:T(128)} %copy-done.17) | copy-start | bytes 772
  506.4 484.6 %copy-start.20 = (f32[64]{0:T(128)S(1)}, f32[64]{0:T(128)}, u32[]{:S(2)}) copy-start(f32[64]{0:T(128)} %copy-done.19) | copy-start | bytes 772
  832.9 158.1 %copy-start.7 = (f32[64,384]{1,0:T(8,128)S(1)}, f32[64,384]{1,0:T(8,128)}, u32[]{:S(2)}) copy-start(f32[64,384]{1,0:T(8,128)} %copy.36) | copy-start | bytes 294916
  832.9 158.1 %copy-start.12 = (f32[64,384]{1,0:T(8,128)S(1)}, f32[64,384]{1,0:T(8,128)}, u32[]{:S(2)}) copy-start(f32[64,384]{1,0:T(8,128)} %copy-done.11) | copy-start | bytes 294916
  832.9 158.1 %copy-start.13 = (f32[64,384]{1,0:T(8,128)S(1)}, f32[64,384]{1,0:T(8,128)}, u32[]{:S(2)}) copy-start(f32[64,384]{1,0:T(8,128)} %get-tuple-element.20) | copy-start | bytes 294916
Sparse Core Ops, SparseCore 0:
  98.6 100.9 all-gather.1
  331.7 156.8 all-reduce.4
  501.3 328.5 all-reduce.8
  835.2 155.7 all-reduce.6
where the time goes:
time: 1000 us
  waiting for transfers between devices  627 us (63%)
  blocking collectives  296 us (30%)
  matrix products  31.5 us (3%)
  local copies, waits for them, and re-layouts  17.8 us (2%)
  between operations  14.1 us (1%)
  other arithmetic  12.8 us (1%)
    psum x1, waiting for transfers between devices, local(): summed_keys, summed_values = lax.psum((key_grad, value_grad), 'pb')  323 us
    psum x1, waiting for transfers between devices, local(): lax.psum((jnp.sum(exp_scores, axis=-1), local_numerator.reshape(row_count...  152 us
    psum x1, waiting for transfers between devices, local(): lax.psum(row_terms, 'ka') + exact_product(gate_input_grad, gate_weight.T)  151 us
    all_gather x1, blocking collectives, local(): lax.all_gather(key_weight, 'ka', axis=0, tiled=True)  48 us
    all_gather x1, blocking collectives, local(): lax.all_gather(gate_weight, 'ka', axis=0, tiled=True)  44.9 us
    all_gather x1, blocking collectives, local(): lax.all_gather(output_weight, 'ka', axis=0, tiled=True)  41.9 us
    all_gather x1, blocking collectives, local(): lax.all_gather(query_weight, 'ka', axis=0, tiled=True)  41.4 us
    psum x1, blocking collectives, local(): lax.psum((jnp.sum(exp_scores, axis=-1), local_numerator.reshape(row_count...  41.4 us
  transfers between devices with their start and end apart: 4, of which 3 were waited for; matrix products, arithmetic and copies ran while one was open for 3% of the time, Pallas kernels for 0%

commit v1 on v0

v1 whole, which is shorter than its diff:
```python
import functools

import jax
import jax.numpy as jnp
from jax import lax
from jax.experimental import pallas as pl
from jax.experimental.pallas import tpu as pltpu
from jax.sharding import PartitionSpec as P

MESH = pl.DeviceIdType.MESH
F32 = jnp.float32
BF16 = jnp.bfloat16
EPS = 1e-05
PENALTY = 1000000000.0

ROWS = 64
COLS = 128
HEADS = 16
DIM = 24
D = 384
CP = 128
KA = 16
PB = 32
SCALE = DIM ** (-0.5)
K_T, Q_T, V_T, G_T, O_T = (0, 1, 2), (3, 4, 5), (8, 9, 10), (11, 12, 13), (6, 7, 14)
NEAR = [(a, b) for a in range(4) for b in ((0, 1, -1, 2) if a % 2 == 0 else (0, 1, -1, -2)) if (a, b) != (0, 0)]
NEAR.sort(key=lambda o: min(o[0], 4 - o[0]) + abs(o[1]))


def nt(a, b):
    return lax.dot_general(a, b, (((1,), (1,)), ((), ())), preferred_element_type=F32)


def tn(a, b):
    return lax.dot_general(a, b, (((0,), (0,)), ((), ())), preferred_element_type=F32)


def nn(a, b):
    return jnp.dot(a, b, preferred_element_type=F32)


def split2(v):
    hi = v.astype(BF16)
    return hi, (v - hi.astype(F32)).astype(BF16)


def kernel(
    single_ref, pair_hbm, mask_ref, ocot_ref, wq_ref, qb_ref, wk_ref, wv_ref, wg_ref, wo_ref, pw_ref,
    out_ref, sgrad_ref, pgrad_hbm,
    xp, nrm, invb, bias, sgp, a_i, nsg, isg, xall, wsend, wall, wfull, qbig, gbig, gate_s, cot_s,
    ebuf, dpbuf, sgb, pbb, stats, stat_send, kg_send, kg_recv, qg_send, qg_recv, fin_send, fin_recv, outb,
    in_sem, out_sem, x_ss, x_rs, w_ss, w_rs, f_ss, f_rs, s_ss, s_rs, k_ss, k_rs, q_ss, q_rs, o_ss, o_rs, loc_sem,
):
    p = lax.axis_index("pb")
    k = lax.axis_index("ka")
    core = lax.rem(p, 2)
    y = lax.rem(lax.div(p, 2), 8)
    x = lax.div(k, 4)
    z = lax.div(p, 16) * 4 + lax.rem(k, 4)
    sib = (p + 1 - 2 * core, k)
    own = lax.div(p, 2)
    quarter = lax.div(k, 4)
    rgroup = lax.rem(k, 4)

    def at(x2, z2):
        x2 = lax.rem(x2 + 4, 4)
        z2 = lax.rem(z2 + 8, 8)
        return ((lax.div(z2, 4) * 8 + y) * 2 + core, x2 * 4 + lax.rem(z2, 4))

    def ka_peer(o):
        return (p, lax.rem(k + o, KA))

    def x_target(o):
        return (quarter * 8 + lax.rem(p + o, 8), own)

    def x_source(o):
        return (2 * k + lax.div(o, 4), lax.div(p, 8) * 4 + lax.rem(o, 4))

    def pair_in(n):
        return pltpu.make_async_copy(pair_hbm.at[pl.ds(n * 16, 16)], xp.at[pl.ds(n * 16, 16)], in_sem.at[n])

    for n in range(4):
        pair_in(n).start()

    bar = pltpu.get_barrier_semaphore()
    for a, b in NEAR:
        pl.semaphore_signal(bar, inc=1, device_id=at(x - a, z - b), device_id_type=MESH)

    def greet_ka(o, c):
        pl.semaphore_signal(bar, inc=1, device_id=ka_peer(o), device_id_type=MESH)
        return c

    lax.fori_loop(1, KA, greet_ka, 0)
    pl.semaphore_signal(bar, inc=1, device_id=sib, device_id_type=MESH)

    def greet_x(o, c):
        src = x_source(o)

        @pl.when(jnp.logical_or(src[0] != p, src[1] != k))
        def _():
            pl.semaphore_signal(bar, inc=1, device_id=src, device_id_type=MESH)

        return c

    lax.fori_loop(0, 8, greet_x, 0)

    sv = single_ref[...].astype(F32)
    cen = sv - jnp.mean(sv, axis=-1, keepdims=True)
    inv = lax.rsqrt(jnp.mean(cen * cen, axis=-1, keepdims=True) + EPS)
    normed = cen * inv
    nsg[...] = normed
    isg[...] = jnp.broadcast_to(inv, (ROWS, 128))
    a_i[...] = normed.astype(BF16).reshape(4, 16, D)

    for ref, tiles in ((wk_ref, K_T), (wq_ref, Q_T), (wv_ref, V_T), (wg_ref, G_T), (wo_ref, O_T)):
        for n, t in enumerate(tiles):
            wsend[t] = ref[:, n * 128 : (n + 1) * 128]
    wsend[15] = jnp.zeros((24, 128), BF16)
    wall[k] = wsend[...]

    self_x = own == k
    pl.semaphore_wait(bar, 15 + 15 + 1 + 8 - self_x.astype(jnp.int32))

    x_slot = lax.rem(p, 2) * 4 + rgroup

    def x_copy(o):
        return pltpu.make_async_remote_copy(
            src_ref=a_i.at[rgroup], dst_ref=xall.at[x_slot], send_sem=x_ss.at[o], recv_sem=x_rs,
            device_id=x_target(o), device_id_type=MESH)

    def x_self():
        return pltpu.make_async_copy(a_i.at[rgroup], xall.at[x_slot], x_rs)

    @pl.when(self_x)
    def _():
        x_self().start()

    @pl.when(jnp.logical_not(self_x))
    def _():
        x_copy(0).start()

    def x_send(o, c):
        x_copy(o).start()
        return c

    lax.fori_loop(1, 8, x_send, 0)

    half = pl.ds(core * 8, 8)

    def w_copy(o):
        a, b = NEAR[o]
        return pltpu.make_async_remote_copy(
            src_ref=wsend.at[half], dst_ref=wall.at[k, half], send_sem=w_ss.at[o], recv_sem=w_rs.at[o],
            device_id=at(x + a, z + b), device_id_type=MESH)

    for o in range(15):
        w_copy(o).start()

    pwv = pw_ref[...].astype(F32)
    pwt = pwv.T
    pwt_b = pwt.astype(BF16)

    def pair_body(i, c):
        v = xp[i].astype(F32)
        cv = v - jnp.mean(v, axis=-1, keepdims=True)
        iv = lax.rsqrt(jnp.mean(cv * cv, axis=-1, keepdims=True) + EPS)
        n = cv * iv
        nrm[i] = n
        invb[i] = jnp.broadcast_to(iv, (COLS, 128))
        hi = n.astype(BF16)
        r = n - hi.astype(F32)
        mid = r.astype(BF16)
        lo = (r - mid.astype(F32)).astype(BF16)
        bias[pl.ds(pl.multiple_of(i * 16, 16), 16), :] = nt(pwt_b, hi) + (nt(pwt_b, mid) + nt(pwt_b, lo))
        return c

    for n in range(4):
        pair_in(n).wait()
        lax.fori_loop(n * 16, (n + 1) * 16, pair_body, 0, unroll=2)

    def f_copy(o):
        a, b = NEAR[o]
        src = at(x - a, z - b)[1]
        return pltpu.make_async_remote_copy(
            src_ref=wall.at[src, half], dst_ref=wall.at[src, half], send_sem=f_ss.at[o], recv_sem=f_rs.at[o],
            device_id=sib, device_id_type=MESH)

    for o in range(15):
        w_copy(o).wait_recv()
        f_copy(o).start()

    pltpu.make_async_copy(xall, xall, x_rs).wait()
    for o in range(15):
        f_copy(o).wait_recv()

    for n, tiles in enumerate((K_T, Q_T, V_T, G_T, O_T)):
        for m, t in enumerate(tiles):
            wfull[n, :, m * 128 : (m + 1) * 128] = wall[:, t].astype(F32).reshape(D, 128).astype(BF16)

    keys_in = xall[...].reshape(COLS, D)
    rows_in = a_i[...].reshape(ROWS, D)
    keys = nn(keys_in, wfull[0]).astype(BF16)
    values = nn(keys_in, wfull[2]).astype(BF16)
    queries = (nn(rows_in, wfull[1]) + qb_ref[...].astype(F32).reshape(1, D)).astype(BF16)
    gate = jax.nn.sigmoid(nn(rows_in, wfull[3]))
    cot = nt(ocot_ref[...], wfull[4])
    gate_s[...] = gate
    cot_s[...] = cot
    agrad = (gate * cot).astype(BF16)

    lane_head = lax.div(lax.broadcasted_iota(jnp.int32, (1, D), 1), DIM)
    heads_f = [jnp.where(lane_head == h, 1.0, 0.0).astype(F32) for h in range(HEADS)]
    for h in range(HEADS):
        mask_b = heads_f[h].astype(BF16)
        qbig[h * ROWS : (h + 1) * ROWS, :] = queries * mask_b
        gbig[h * ROWS : (h + 1) * ROWS, :] = agrad * mask_b

    pen = (mask_ref[...].astype(F32).reshape(1, COLS) - 1.0) * PENALTY
    lane = lax.broadcasted_iota(jnp.int32, (8, 128), 1)
    pm = jnp.zeros((8, 128), F32)
    pt = jnp.zeros((8, 128), F32)
    pd = jnp.zeros((8, 128), F32)
    for h in range(HEADS):
        rows = slice(h * ROWS, (h + 1) * ROWS)
        logits = nt(qbig[rows, :], keys) * SCALE + bias[pl.ds(h, ROWS, stride=HEADS), :] + pen
        dp = nt(gbig[rows, :], values)
        mx = jnp.max(logits, axis=-1, keepdims=True)
        e = jnp.exp(logits - mx)
        ebuf[rows, :] = e
        dpbuf[rows, :] = dp
        tot = jnp.sum(e, axis=-1, keepdims=True)
        dd = jnp.sum(e * dp, axis=-1, keepdims=True)
        for g in range(8):
            here = lane == g * 16 + h
            s8 = slice(g * 8, g * 8 + 8)
            pm = jnp.where(here, mx[s8], pm)
            pt = jnp.where(here, tot[s8], pt)
            pd = jnp.where(here, dd[s8], pd)
    stat_send[0:8, :] = pm
    stat_send[8:16, :] = pt
    stat_send[16:24, :] = pd

    def s_copy(o):
        return pltpu.make_async_remote_copy(
            src_ref=stat_send, dst_ref=stats.at[k], send_sem=s_ss.at[o], recv_sem=s_rs,
            device_id=ka_peer(o), device_id_type=MESH)

    def s_start(o, c):
        s_copy(o).start()
        return c

    lax.fori_loop(1, KA, s_start, 0)
    pltpu.make_async_copy(stat_send, stats.at[k], s_rs).start()
    pltpu.make_async_copy(stats, stats, s_rs).wait()

    st = stats[...]
    all_m, all_t, all_d = st[:, 0:8], st[:, 8:16], st[:, 16:24]
    gm = jnp.max(all_m, axis=0)
    wts = jnp.exp(all_m - gm[None])
    gt = jnp.sum(wts * all_t, axis=0)
    gd = jnp.sum(wts * all_d, axis=0)
    coef = jnp.exp(pm - gm) / gt
    delta = gd / gt

    for h in range(HEADS):
        rows = slice(h * ROWS, (h + 1) * ROWS)
        cc = jnp.concatenate([jnp.broadcast_to(coef[:, g * 16 + h : g * 16 + h + 1], (8, 128)) for g in range(8)], axis=0)
        dc = jnp.concatenate([jnp.broadcast_to(delta[:, g * 16 + h : g * 16 + h + 1], (8, 128)) for g in range(8)], axis=0)
        prob = ebuf[rows, :] * cc
        sg = prob * (dpbuf[rows, :] - dc)
        sgp[pl.ds(h, ROWS, stride=HEADS), :] = sg
        sgb[rows, :] = sg.astype(BF16)
        pbb[rows, :] = prob.astype(BF16)

    kg = tn(sgb[...], qbig[...]) * SCALE
    vg = tn(pbb[...], gbig[...])
    for c in range(2):
        for t in range(8):
            r8 = slice(c * 64 + t * 8, c * 64 + t * 8 + 8)
            kg_send[c * 8 + t] = jnp.concatenate([kg[r8], vg[r8]], axis=0).astype(BF16)

    def k_dest(n):
        c, t = lax.div(n, 8), lax.rem(n, 8)
        return (2 * k + c, 2 * t + c)

    def k_copy(n):
        return pltpu.make_async_remote_copy(
            src_ref=kg_send.at[n], dst_ref=kg_recv.at[p], send_sem=k_ss.at[n], recv_sem=k_rs,
            device_id=k_dest(n), device_id_type=MESH)

    def k_start(n, c):
        d = k_dest(n)
        mine = jnp.logical_and(d[0] == p, d[1] == k)

        @pl.when(mine)
        def _():
            pltpu.make_async_copy(kg_send.at[n], kg_recv.at[p], k_rs).start()

        @pl.when(jnp.logical_not(mine))
        def _():
            k_copy(n).start()

        return c

    lax.fori_loop(0, 16, k_start, 0)

    qg = jnp.zeros((ROWS, D), F32)
    att = jnp.zeros((ROWS, D), F32)
    for h in range(HEADS):
        rows = slice(h * ROWS, (h + 1) * ROWS)
        qg = qg + nn(sgb[rows, :], keys) * heads_f[h]
        att = att + nn(pbb[rows, :], values) * heads_f[h]
    qg = qg * SCALE
    for t in range(8):
        r8 = slice(t * 8, t * 8 + 8)
        qg_send[t] = jnp.concatenate([qg[r8], att[r8]], axis=0).astype(BF16)

    def q_copy(t):
        return pltpu.make_async_remote_copy(
            src_ref=qg_send.at[t], dst_ref=qg_recv.at[k], send_sem=q_ss.at[t], recv_sem=q_rs,
            device_id=(p, 2 * t + core), device_id_type=MESH)

    def q_start(t, c):
        mine = 2 * t + core == k

        @pl.when(mine)
        def _():
            pltpu.make_async_copy(qg_send.at[t], qg_recv.at[k], q_rs).start()

        @pl.when(jnp.logical_not(mine))
        def _():
            q_copy(t).start()

        return c

    lax.fori_loop(0, 8, q_start, 0)

    wc = pwt - jnp.mean(pwt, axis=-1, keepdims=True)
    wc_hi, wc_lo = split2(wc)
    zero16 = jnp.zeros((16, 128), BF16)
    ones8 = jnp.where(lax.broadcasted_iota(jnp.int32, (16, 128), 0) < 2, 1.0, 0.0).astype(BF16)
    rhs = jnp.concatenate(
        [jnp.concatenate([wc_hi, wc_hi, wc_lo, zero16], axis=0), jnp.concatenate([zero16, zero16, zero16, ones8], axis=0)], axis=1)
    row16 = lax.broadcasted_iota(jnp.int32, (16, 128), 0)

    def grad_body(i, c):
        r16 = pl.ds(pl.multiple_of(i * 16, 16), 16)
        sg = sgp[r16, :]
        s = jnp.sum(sg * bias[r16, :], axis=0, keepdims=True) * (1.0 / CP)
        hi, lo = split2(sg)
        s_hi = s.astype(BF16).astype(F32)
        s2 = jnp.where(row16 == 0, s_hi, jnp.where(row16 == 1, s - s_hi, 0.0)).astype(BF16)
        lhs = jnp.concatenate([hi, lo, hi, s2], axis=0)
        both = tn(lhs, rhs)
        outb[i] = (invb[i] * (both[:, :128] - nrm[i] * both[:, 128:])).astype(BF16)
        return c

    def pair_out(n):
        return pltpu.make_async_copy(outb.at[pl.ds(n * 16, 16)], pgrad_hbm.at[pl.ds(n * 16, 16)], out_sem.at[n])

    for n in range(4):
        lax.fori_loop(n * 16, (n + 1) * 16, grad_body, 0, unroll=2)
        pair_out(n).start()

    is_red = lax.rem(k, 2) == core
    t_me = lax.div(k, 2)

    def o_copy(o):
        return pltpu.make_async_remote_copy(
            src_ref=fin_send, dst_ref=fin_recv.at[t_me], send_sem=o_ss.at[o], recv_sem=o_rs,
            device_id=ka_peer(o), device_id_type=MESH)

    @pl.when(is_red)
    def _():
        pltpu.make_async_copy(qg_recv, qg_recv, q_rs).wait()
        pltpu.make_async_copy(kg_recv, kg_recv, k_rs).wait()
        kv = jnp.sum(kg_recv[...].astype(F32), axis=0)
        qa = jnp.sum(qg_recv[...].astype(F32), axis=0)
        r8 = pl.ds(pl.multiple_of(t_me * 8, 8), 8)
        g8 = gate_s[r8, :]
        att8 = qa[8:16]
        gig = cot_s[r8, :] * att8 * g8 * (1.0 - g8)
        grads = (kv[0:8], qa[0:8], kv[8:16], gig)
        ig = jnp.zeros((8, D), F32)
        for n, gr in enumerate(grads):
            hi, lo = split2(gr)
            two = nt(jnp.concatenate([hi.astype(F32), lo.astype(F32)], axis=0).astype(BF16), wfull[n])
            ig = ig + (two[0:8] + two[8:16])
        n8 = nsg[r8, :]
        sgr = isg[r8, 0:1] * (
            ig - jnp.mean(ig, axis=-1, keepdims=True) - n8 * jnp.mean(ig * n8, axis=-1, keepdims=True))
        gated = g8 * att8
        ao = nn(jnp.concatenate([gated, gated], axis=0).astype(BF16), wfull[4])[0:8]
        fin_send[...] = jnp.concatenate([sgr, ao], axis=0).astype(BF16)

        def o_start(o, c):
            o_copy(o).start()
            return c

        lax.fori_loop(1, KA, o_start, 0)
        pltpu.make_async_copy(fin_send, fin_recv.at[t_me], o_rs).start()

    pltpu.make_async_copy(fin_recv, fin_recv, o_rs).wait()
    fin = fin_recv[...].astype(F32)
    sgrad_ref[...] = fin[:, 0:8].reshape(ROWS, D).astype(BF16)
    out_ref[...] = fin[:, 8:16].reshape(ROWS, D).astype(BF16)

    @pl.when(jnp.logical_not(self_x))
    def _():
        x_copy(0).wait_send()

    def x_done(o, c):
        x_copy(o).wait_send()
        return c

    lax.fori_loop(1, 8, x_done, 0)
    for o in range(15):
        w_copy(o).wait_send()
        f_copy(o).wait_send()

    def s_done(o, c):
        s_copy(o).wait_send()
        return c

    lax.fori_loop(1, KA, s_done, 0)

    def k_done(n, c):
        d = k_dest(n)

        @pl.when(jnp.logical_or(d[0] != p, d[1] != k))
        def _():
            k_copy(n).wait_send()

        return c

    lax.fori_loop(0, 16, k_done, 0)

    def q_done(t, c):
        @pl.when(2 * t + core != k)
        def _():
            q_copy(t).wait_send()

        return c

    lax.fori_loop(0, 8, q_done, 0)

    @pl.when(is_red)
    def _():
        def o_done(o, c):
            o_copy(o).wait_send()
            return c

        lax.fori_loop(1, KA, o_done, 0)

    for n in range(4):
        pair_out(n).wait()


def local(*args):
    vmem = pl.BlockSpec(memory_space=pltpu.VMEM)
    hbm = pl.BlockSpec(memory_space=pl.ANY)
    dma = pltpu.SemaphoreType.DMA
    big = (ROWS, COLS, CP)
    flat = (HEADS * ROWS, 128)
    return pl.pallas_call(
        kernel,
        out_shape=(
            jax.ShapeDtypeStruct((ROWS, D), BF16),
            jax.ShapeDtypeStruct((ROWS, D), BF16),
            jax.ShapeDtypeStruct(big, BF16),
        ),
        in_specs=[vmem, hbm] + [vmem] * 9,
        out_specs=(vmem, vmem, hbm),
        scratch_shapes=[
            pltpu.VMEM(big, BF16),
            pltpu.VMEM(big, F32),
            pltpu.VMEM(big, F32),
            pltpu.VMEM(flat, F32),
            pltpu.VMEM(flat, F32),
            pltpu.VMEM((4, 16, D), BF16),
            pltpu.VMEM((ROWS, D), F32),
            pltpu.VMEM((ROWS, 128), F32),
            pltpu.VMEM((8, 16, D), BF16),
            pltpu.VMEM((16, 24, 128), BF16),
            pltpu.VMEM((KA, 16, 24, 128), BF16),
            pltpu.VMEM((5, D, D), BF16),
            pltpu.VMEM((HEADS * ROWS, D), BF16),
            pltpu.VMEM((HEADS * ROWS, D), BF16),
            pltpu.VMEM((ROWS, D), F32),
            pltpu.VMEM((ROWS, D), F32),
            pltpu.VMEM(flat, F32),
            pltpu.VMEM(flat, F32),
            pltpu.VMEM(flat, BF16),
            pltpu.VMEM(flat, BF16),
            pltpu.VMEM((KA, 24, 128), F32),
            pltpu.VMEM((24, 128), F32),
            pltpu.VMEM((16, 16, D), BF16),
            pltpu.VMEM((PB, 16, D), BF16),
            pltpu.VMEM((8, 16, D), BF16),
            pltpu.VMEM((KA, 16, D), BF16),
            pltpu.VMEM((16, D), BF16),
            pltpu.VMEM((8, 16, D), BF16),
            pltpu.VMEM(big, BF16),
            dma((4,)), dma((4,)),
            dma((8,)), dma,
            dma((15,)), dma((15,)),
            dma((15,)), dma((15,)),
            dma((16,)), dma,
            dma((16,)), dma,
            dma((8,)), dma,
            dma((16,)), dma,
            dma,
        ],
        compiler_params=pltpu.CompilerParams(
            collective_id=0, has_side_effects=True, vmem_limit_bytes=48 * 1024 * 1024),
    )(*args)


def solution(mesh):
    in_specs = (
        P("pb", None), P("pb", "ka", None), P("ka"), P("pb", None), P("ka", None), P(),
        P("ka", None), P("ka", None), P("ka", None), P("ka", None), P(),
    )
    out_specs = (P("pb", None), P("pb", None), P("pb", "ka", None))
    return jax.shard_map(local, mesh=mesh, in_specs=in_specs, out_specs=out_specs, check_vma=False)
```

time: 1000 us -> 93 us (0.09)
  the two profiles are of different devices: /device:TPU:56 before, /device:TPU:1 now
where the time goes in v1:
time: 93 us; the launch traced here: 92.4 us
  Pallas kernels  80.3 us (86%)
  local copies, waits for them, and re-layouts  11.5 us (12%)
    pallas_call x1, Pallas kernels, local(): pl.pallas_call(kernel, out_shape=(jax.ShapeDtypeStruct((ROWS, D), BF16),...  80.3 us
    unnamed x24, local copies, waits for them, and re-layouts  11.5 us

profile of v1, /device:TPU:1, one launch (start us, length us, event | category | flops | bytes accessed | tf_op | source)
XLA Modules:
  0.0 92.4 jit_solution(2027132682040091147)
XLA Ops:
  0.6 0.8 copy.14.pw_ref
  1.4 0.0 copy-start
  1.4 1.6 %copy-done = bf16[64,128,128]{2,1,0:T(8,128)(2,1)S(1)} copy-done((bf16[64,128,128]{2,1,0:T(8,128)(2,1)S(1)}, bf16[64,128,128]{2,1,0:T(8,128)(2,1)}, u32[]{:S(2)}) %copy-start) | copy-done | bytes 2097176
  3.0 0.0 copy-start.1
  3.0 0.8 copy-done.1
  3.8 0.0 copy-start.2
  3.8 0.8 copy-done.2
  4.6 0.0 copy-start.3
  4.6 0.7 copy-done.3
  5.3 0.0 copy-start.4
  5.4 0.7 copy-done.4
  6.1 0.0 copy-start.5
  6.1 0.7 copy-done.5
  6.8 0.0 copy-start.6
  6.8 0.7 copy-done.6
  7.5 0.0 copy-start.7
  7.5 0.7 copy-done.7
  8.2 0.0 copy-start.8
  8.2 0.7 copy-done.8
  8.9 0.0 copy-start.9
  8.9 0.7 copy-done.9
  9.6 80.3 %shard_map.130 = (bf16[64,384]{1,0:T(8,128)(2,1)S(1)}, bf16[64,384]{1,0:T(8,128)(2,1)S(1)}, bf16[64,128,128]{2,1,0:T(8,128)(2,1)S(1)}) custom-call(bf16[64,384]{1,0:T(8,128)(2,1)S(1)} %copy-done.1, bf16[64,128,128]{2,1,0:T(8,128)(2,1)S(1)} %copy-done, s32[128]{0:T(128)S(1)} %copy-done.9, bf16[64,384]{1,0:T(8,128)(2,1)S(1)} %copy-done.2, ...), custom_call_target="tpu_custom_call" | custom-call | tf_op jit(solution)/shard_map/pallas_call | solution.py:465
  89.9 0.6 copy.18
  90.5 0.6 copy.19
  91.1 1.3 %copy.20 = bf16[64,128,128]{2,1,0:T(8,128)(2,1)} copy(bf16[64,128,128]{2,1,0:T(8,128)(2,1)S(1)} %get-tuple-element.8) | data formatting | bytes 4194304
Async XLA Ops:
  1.4 1.6 %copy-start = (bf16[64,128,128]{2,1,0:T(8,128)(2,1)S(1)}, bf16[64,128,128]{2,1,0:T(8,128)(2,1)}, u32[]{:S(2)}) copy-start(bf16[64,128,128]{2,1,0:T(8,128)(2,1)} %pair_hbm.1) | copy-start | bytes 6291460
  3.0 0.8 copy-start.1
  3.8 0.8 copy-start.2
  4.6 0.7 copy-start.3
  5.3 0.7 copy-start.4
  6.1 0.7 copy-start.5
  6.8 0.7 copy-start.6
  7.5 0.7 copy-start.7
  8.2 0.7 copy-start.8
  8.9 0.7 copy-start.9

commit v2 on v1

v2 whole, which is shorter than its diff:
```python
import functools

import jax
import jax.numpy as jnp
from jax import lax
from jax.experimental import pallas as pl
from jax.experimental.pallas import tpu as pltpu
from jax.sharding import PartitionSpec as P

MESH = pl.DeviceIdType.MESH
F32 = jnp.float32
BF16 = jnp.bfloat16
EPS = 1e-05
PENALTY = 1000000000.0

ROWS = 64
COLS = 128
HEADS = 16
DIM = 24
D = 384
CP = 128
KA = 16
PB = 32
SCALE = DIM ** (-0.5)
K_T, Q_T, V_T, G_T, O_T = (0, 1, 2), (3, 4, 5), (8, 9, 10), (11, 12, 13), (6, 7, 14)
NEAR = [(a, b) for a in range(4) for b in ((0, 1, -1, 2) if a % 2 == 0 else (0, 1, -1, -2)) if (a, b) != (0, 0)]
NEAR.sort(key=lambda o: min(o[0], 4 - o[0]) + abs(o[1]))


def nt(a, b):
    return lax.dot_general(a, b, (((1,), (1,)), ((), ())), preferred_element_type=F32)


def tn(a, b):
    return lax.dot_general(a, b, (((0,), (0,)), ((), ())), preferred_element_type=F32)


def nn(a, b):
    return jnp.dot(a, b, preferred_element_type=F32)


def split2(v):
    hi = v.astype(BF16)
    return hi, (v - hi.astype(F32)).astype(BF16)


def kernel(
    single_hbm, pair_hbm, mask_hbm, ocot_hbm, wq_hbm, qb_hbm, wk_hbm, wv_hbm, wg_hbm, wo_hbm, pw_hbm,
    out_ref, sgrad_ref, pgrad_hbm,
    outb,    single_ref, mask_ref, ocot_ref, qb_ref, pw_ref, xp, nrm, invb, bias, sgp, a_i, nsg, isg, xall, wsend, wall, wfull, qbig, gbig, gate_s, cot_s,
    ebuf, dpbuf, sgb, pbb, stats, stat_send, kv_half, kv_other, kg_send, kg_recv, qg_send, qg_recv, fin_send, fin_recv,
    in_sem, out_sem, small_sem, wl_sem, x_ss, x_rs, xf_ss, xf_rs, w_ss, w_rs, f_ss, f_rs, s_ss, s_rs, h_ss, h_rs, k_ss, k_rs, q_ss, q_rs, o_ss, o_rs,
):
    p = lax.axis_index("pb")
    k = lax.axis_index("ka")
    core = lax.rem(p, 2)
    y = lax.rem(lax.div(p, 2), 8)
    x = lax.div(k, 4)
    z = lax.div(p, 16) * 4 + lax.rem(k, 4)
    sib = (p + 1 - 2 * core, k)
    own = lax.div(p, 2)
    quarter = lax.div(k, 4)
    rgroup = lax.rem(k, 4)
    chip = lax.div(p, 2)

    def at(x2, z2):
        x2 = lax.rem(x2 + 4, 4)
        z2 = lax.rem(z2 + 8, 8)
        return ((lax.div(z2, 4) * 8 + y) * 2 + core, x2 * 4 + lax.rem(z2, 4))

    def ka_peer(o):
        return (p, lax.rem(k + o, KA))

    def x_target(o):
        return (quarter * 8 + lax.rem(p + 2 * o, 8), own)

    def x_source(o):
        return (2 * k + core, lax.div(p, 8) * 4 + o)

    def pair_in(n):
        return pltpu.make_async_copy(pair_hbm.at[pl.ds(n * 16, 16)], xp.at[pl.ds(n * 16, 16)], in_sem.at[n])

    single_in = pltpu.make_async_copy(single_hbm, single_ref, small_sem.at[0])
    single_in.start()
    weights_in = [
        pltpu.make_async_copy(ref.at[:, pl.ds(n * 128, 128)], wsend.at[t], wl_sem.at[t])
        for ref, tiles in ((wk_hbm, K_T), (wq_hbm, Q_T), (wv_hbm, V_T), (wg_hbm, G_T), (wo_hbm, O_T))
        for n, t in enumerate(tiles)
    ]
    for copy in weights_in:
        copy.start()
    small_in = [
        pltpu.make_async_copy(src, dst, small_sem.at[n + 1])
        for n, (src, dst) in enumerate(((mask_hbm, mask_ref), (ocot_hbm, ocot_ref), (qb_hbm, qb_ref), (pw_hbm, pw_ref)))
    ]
    for copy in small_in:
        copy.start()
    for n in range(4):
        pair_in(n).start()

    bar = pltpu.get_barrier_semaphore()
    for a, b in NEAR:
        pl.semaphore_signal(bar, inc=1, device_id=at(x - a, z - b), device_id_type=MESH)

    def greet_ka(o, c):
        pl.semaphore_signal(bar, inc=1, device_id=ka_peer(o), device_id_type=MESH)
        return c

    lax.fori_loop(1, KA, greet_ka, 0)
    pl.semaphore_signal(bar, inc=1, device_id=sib, device_id_type=MESH)

    def greet_x(o, c):
        src = x_source(o)

        @pl.when(jnp.logical_or(src[0] != p, src[1] != k))
        def _():
            pl.semaphore_signal(bar, inc=1, device_id=src, device_id_type=MESH)

        return c

    lax.fori_loop(0, 4, greet_x, 0)

    single_in.wait()
    sv = single_ref[...].astype(F32)
    cen = sv - jnp.mean(sv, axis=-1, keepdims=True)
    inv = lax.rsqrt(jnp.mean(cen * cen, axis=-1, keepdims=True) + EPS)
    normed = cen * inv
    nsg[...] = normed
    isg[...] = jnp.broadcast_to(inv, (ROWS, 128))
    a_i[...] = normed.astype(BF16).reshape(4, 16, D)

    for copy in weights_in:
        copy.wait()
    wsend[15] = jnp.zeros((24, 128), BF16)
    wall[k] = wsend[...]

    self_x = own == k
    pl.semaphore_wait(bar, 15 + 15 + 1 + 4 - self_x.astype(jnp.int32))

    def x_copy(o):
        return pltpu.make_async_remote_copy(
            src_ref=a_i.at[rgroup], dst_ref=xall.at[core, rgroup], send_sem=x_ss.at[o], recv_sem=x_rs,
            device_id=x_target(o), device_id_type=MESH)

    def x_self():
        return pltpu.make_async_copy(a_i.at[rgroup], xall.at[core, rgroup], x_rs)

    @pl.when(self_x)
    def _():
        x_self().start()

    @pl.when(jnp.logical_not(self_x))
    def _():
        x_copy(0).start()

    def x_send(o, c):
        x_copy(o).start()
        return c

    lax.fori_loop(1, 4, x_send, 0)

    half = pl.ds(core * 8, 8)

    def w_copy(o):
        a, b = NEAR[o]
        return pltpu.make_async_remote_copy(
            src_ref=wsend.at[half], dst_ref=wall.at[k, half], send_sem=w_ss.at[o], recv_sem=w_rs.at[o],
            device_id=at(x + a, z + b), device_id_type=MESH)

    for o in range(15):
        w_copy(o).start()

    for copy in small_in:
        copy.wait()
    pwt_b = pw_ref[...]
    pwt = pwt_b.astype(F32)

    mean_w = jnp.full((CP, CP), 1.0 / CP, BF16)

    def pair_body(n, c):
        i8 = pl.ds(pl.multiple_of(n * 8, 8), 8)
        vb = xp[i8].reshape(8 * COLS, CP)
        v = vb.astype(F32)
        cv = v - nn(vb, mean_w)
        sq_hi, sq_lo = split2(cv * cv)
        iv = lax.rsqrt(nn(sq_hi, mean_w) + nn(sq_lo, mean_w) + EPS)
        nv = cv * iv
        nrm[i8] = nv.reshape(8, COLS, CP)
        invb[i8] = iv.reshape(8, COLS, CP)
        hi, mid = split2(nv)
        both = nt(pwt_b, hi) + nt(pwt_b, mid)
        for m in range(8):
            bias[pl.ds(pl.multiple_of(n * 128 + m * 16, 16), 16), :] = both[:, m * 128 : (m + 1) * 128]
        return c

    for n in range(4):
        pair_in(n).wait()
        lax.fori_loop(n * 2, n * 2 + 2, pair_body, 0)

    def f_copy(o):
        a, b = NEAR[o]
        src = at(x - a, z - b)[1]
        return pltpu.make_async_remote_copy(
            src_ref=wall.at[src, half], dst_ref=wall.at[src, half], send_sem=f_ss.at[o], recv_sem=f_rs.at[o],
            device_id=sib, device_id_type=MESH)

    for o in range(15):
        w_copy(o).wait_recv()
        f_copy(o).start()

    pltpu.make_async_copy(xall.at[core], xall.at[core], x_rs).wait()
    x_fwd = pltpu.make_async_remote_copy(
        src_ref=xall.at[core], dst_ref=xall.at[core], send_sem=xf_ss, recv_sem=xf_rs,
        device_id=sib, device_id_type=MESH)
    x_fwd.start()

    def build(first):
        for n in range(8):
            wfull[first + n] = wall[:, first + n].astype(F32).reshape(D, 128).astype(BF16)

    build(core * 8)
    for o in range(15):
        f_copy(o).wait_recv()
    build(8 - core * 8)
    x_fwd.wait_recv()

    def weight(tiles):
        return jnp.concatenate([wfull[t] for t in tiles], axis=1)

    keys_in = xall[...].reshape(COLS, D)
    rows_in = a_i[...].reshape(ROWS, D)
    keys = nn(keys_in, weight(K_T)).astype(BF16)
    values = nn(keys_in, weight(V_T)).astype(BF16)
    queries = (nn(rows_in, weight(Q_T)) + qb_ref[...].astype(F32).reshape(1, D)).astype(BF16)
    gate = jax.nn.sigmoid(nn(rows_in, weight(G_T)))
    cot = nt(ocot_ref[...], weight(O_T))
    gate_s[...] = gate
    cot_s[...] = cot
    agrad = (gate * cot).astype(BF16)

    lane_head = lax.div(lax.broadcasted_iota(jnp.int32, (1, D), 1), DIM)
    heads_f = [jnp.where(lane_head == h, 1.0, 0.0).astype(F32) for h in range(HEADS)]
    for h in range(HEADS):
        mask_b = heads_f[h].astype(BF16)
        qbig[h * ROWS : (h + 1) * ROWS, :] = queries * mask_b
        gbig[h * ROWS : (h + 1) * ROWS, :] = agrad * mask_b

    pen = (mask_ref[...].astype(F32).reshape(1, COLS) - 1.0) * PENALTY
    lane = lax.broadcasted_iota(jnp.int32, (8, 128), 1)
    pm = jnp.zeros((8, 128), F32)
    pt = jnp.zeros((8, 128), F32)
    pd = jnp.zeros((8, 128), F32)
    for h in range(HEADS):
        rows = slice(h * ROWS, (h + 1) * ROWS)
        logits = nt(qbig[rows, :], keys) * SCALE + bias[pl.ds(h, ROWS, stride=HEADS), :] + pen
        dp = nt(gbig[rows, :], values)
        mx = jnp.max(logits, axis=-1, keepdims=True)
        e = jnp.exp(logits - mx)
        ebuf[rows, :] = e
        dpbuf[rows, :] = dp
        tot = jnp.sum(e, axis=-1, keepdims=True)
        dd = jnp.sum(e * dp, axis=-1, keepdims=True)
        for g in range(8):
            here = lane == g * 16 + h
            s8 = slice(g * 8, g * 8 + 8)
            pm = jnp.where(here, mx[s8], pm)
            pt = jnp.where(here, tot[s8], pt)
            pd = jnp.where(here, dd[s8], pd)
    stat_send[0:8, :] = pm
    stat_send[8:16, :] = pt
    stat_send[16:24, :] = pd

    def s_copy(o):
        return pltpu.make_async_remote_copy(
            src_ref=stat_send, dst_ref=stats.at[k], send_sem=s_ss.at[o], recv_sem=s_rs,
            device_id=ka_peer(o), device_id_type=MESH)

    def s_start(o, c):
        s_copy(o).start()
        return c

    lax.fori_loop(1, KA, s_start, 0)
    pltpu.make_async_copy(stat_send, stats.at[k], s_rs).start()
    num = jnp.zeros((ROWS, D), F32)
    for h in range(HEADS):
        rows = slice(h * ROWS, (h + 1) * ROWS)
        num = num + nn(ebuf[rows, :].astype(BF16), values) * heads_f[h]
    pltpu.make_async_copy(stats, stats, s_rs).wait()

    st = stats[...]
    all_m, all_t, all_d = st[:, 0:8], st[:, 8:16], st[:, 16:24]
    gm = jnp.max(all_m, axis=0)
    wts = jnp.exp(all_m - gm[None])
    gt = jnp.sum(wts * all_t, axis=0)
    gd = jnp.sum(wts * all_d, axis=0)
    coef = jnp.exp(pm - gm) / gt
    delta = gd / gt
    coef_f = jnp.zeros((ROWS, D), F32)

    for h in range(HEADS):
        rows = slice(h * ROWS, (h + 1) * ROWS)
        cc = jnp.concatenate([jnp.broadcast_to(coef[:, g * 16 + h : g * 16 + h + 1], (8, 128)) for g in range(8)], axis=0)
        dc = jnp.concatenate([jnp.broadcast_to(delta[:, g * 16 + h : g * 16 + h + 1], (8, 128)) for g in range(8)], axis=0)
        coef_f = coef_f + jnp.concatenate([cc] * 3, axis=1) * heads_f[h]
        prob = ebuf[rows, :] * cc
        sg = prob * (dpbuf[rows, :] - dc)
        sgp[pl.ds(h, ROWS, stride=HEADS), :] = sg
        sgb[rows, :] = sg.astype(BF16)
        pbb[rows, :] = prob.astype(BF16)

    att = num * coef_f

    def back(v, n):
        hi, lo = split2(v)
        w = weight(n)
        return nt(hi, w) + nt(lo, w)

    key_in = back(tn(sgb[...], qbig[...]) * SCALE, K_T) + back(tn(pbb[...], gbig[...]), V_T)
    kv_half[0] = key_in[0:ROWS]
    kv_half[1] = key_in[ROWS : 2 * ROWS]
    h_copy = pltpu.make_async_remote_copy(
        src_ref=kv_half.at[1 - core], dst_ref=kv_other, send_sem=h_ss, recv_sem=h_rs,
        device_id=sib, device_id_type=MESH)
    h_copy.start()

    qg = jnp.zeros((ROWS, D), F32)
    for h in range(HEADS):
        rows = slice(h * ROWS, (h + 1) * ROWS)
        qg = qg + nn(sgb[rows, :], keys) * heads_f[h]
    row_in = back(qg * SCALE, Q_T)
    for t in range(4):
        qg_send[t, 0:16, :] = row_in[t * 16 : t * 16 + 16].astype(BF16)

    h_copy.wait_recv()
    kg_send[...] = (kv_half[core] + kv_other[...]).astype(BF16).reshape(4, 16, D)

    def red_of(t):
        return 4 * t + 1 + core

    def k_copy(t):
        return pltpu.make_async_remote_copy(
            src_ref=kg_send.at[t], dst_ref=kg_recv.at[chip], send_sem=k_ss.at[t], recv_sem=k_rs,
            device_id=(2 * k + core, red_of(t)), device_id_type=MESH)

    def k_mine(t):
        return jnp.logical_and(2 * k + core == p, red_of(t) == k)

    def k_start(t, c):
        mine = k_mine(t)

        @pl.when(mine)
        def _():
            pltpu.make_async_copy(kg_send.at[t], kg_recv.at[chip], k_rs).start()

        @pl.when(jnp.logical_not(mine))
        def _():
            k_copy(t).start()

        return c

    lax.fori_loop(0, 4, k_start, 0)

    for t in range(4):
        qg_send[t, 16:32, :] = att[t * 16 : t * 16 + 16].astype(BF16)

    def q_copy(t):
        return pltpu.make_async_remote_copy(
            src_ref=qg_send.at[t], dst_ref=qg_recv.at[k], send_sem=q_ss.at[t], recv_sem=q_rs,
            device_id=(p, red_of(t)), device_id_type=MESH)

    def q_start(t, c):
        mine = red_of(t) == k

        @pl.when(mine)
        def _():
            pltpu.make_async_copy(qg_send.at[t], qg_recv.at[k], q_rs).start()

        @pl.when(jnp.logical_not(mine))
        def _():
            q_copy(t).start()

        return c

    lax.fori_loop(0, 4, q_start, 0)

    wc = pwt - jnp.mean(pwt, axis=-1, keepdims=True)
    wc_hi, wc_lo = split2(wc)
    zero16 = jnp.zeros((16, 128), BF16)
    ones8 = jnp.where(lax.broadcasted_iota(jnp.int32, (16, 128), 0) < 2, 1.0, 0.0).astype(BF16)
    rhs = jnp.concatenate(
        [jnp.concatenate([wc_hi, wc_hi, wc_lo, zero16], axis=0), jnp.concatenate([zero16, zero16, zero16, ones8], axis=0)], axis=1)
    row16 = lax.broadcasted_iota(jnp.int32, (16, 128), 0)

    def grad_body(i, c):
        r16 = pl.ds(pl.multiple_of(i * 16, 16), 16)
        sg = sgp[r16, :]
        s = jnp.sum(sg * bias[r16, :], axis=0, keepdims=True) * (1.0 / CP)
        hi, lo = split2(sg)
        s_hi = s.astype(BF16).astype(F32)
        s2 = jnp.where(row16 == 0, s_hi, jnp.where(row16 == 1, s - s_hi, 0.0)).astype(BF16)
        lhs = jnp.concatenate([hi, lo, hi, s2], axis=0)
        both = tn(lhs, rhs)
        outb[i] = (invb[i] * (both[:, :128] - nrm[i] * both[:, 128:])).astype(BF16)
        return c

    def pair_out(n):
        return pltpu.make_async_copy(outb.at[pl.ds(n * 16, 16)], pgrad_hbm.at[pl.ds(n * 16, 16)], out_sem.at[n])

    for n in range(4):
        lax.fori_loop(n * 16, (n + 1) * 16, grad_body, 0, unroll=4)
        pair_out(n).start()

    is_red = lax.rem(k, 4) == 1 + core
    t_me = quarter

    def o_copy(o):
        return pltpu.make_async_remote_copy(
            src_ref=fin_send, dst_ref=fin_recv.at[t_me], send_sem=o_ss.at[o], recv_sem=o_rs,
            device_id=ka_peer(o), device_id_type=MESH)

    @pl.when(is_red)
    def _():
        pltpu.make_async_copy(qg_recv, qg_recv, q_rs).wait()
        r16 = pl.ds(pl.multiple_of(t_me * 16, 16), 16)
        qa = jnp.sum(qg_recv[...].astype(F32), axis=0)
        g16 = gate_s[r16, :]
        att16 = qa[16:32]
        gig = cot_s[r16, :] * att16 * g16 * (1.0 - g16)
        part = qa[0:16] + back(gig, G_T)
        fin_send[16:32, :] = nn((g16 * att16).astype(BF16), weight(O_T)).astype(BF16)
        pltpu.make_async_copy(kg_recv, kg_recv, k_rs).wait()
        ig = part + jnp.sum(kg_recv[...].astype(F32), axis=0)
        n16 = nsg[r16, :]
        sgr = isg[r16, 0:1] * (
            ig - jnp.mean(ig, axis=-1, keepdims=True) - n16 * jnp.mean(ig * n16, axis=-1, keepdims=True))
        fin_send[0:16, :] = sgr.astype(BF16)

        def o_start(o, c):
            o_copy(o).start()
            return c

        lax.fori_loop(1, KA, o_start, 0)
        pltpu.make_async_copy(fin_send, fin_recv.at[t_me], o_rs).start()

    pltpu.make_async_copy(fin_recv, fin_recv, o_rs).wait()
    for t in range(4):
        sgrad_ref[t * 16 : t * 16 + 16, :] = fin_recv[t, 0:16, :]
        out_ref[t * 16 : t * 16 + 16, :] = fin_recv[t, 16:32, :]

    for n in range(4):
        pair_out(n).wait()
    x_fwd.wait_send()
    @pl.when(jnp.logical_not(self_x))
    def _():
        x_copy(0).wait_send()

    def x_done(o, c):
        x_copy(o).wait_send()
        return c

    lax.fori_loop(1, 4, x_done, 0)
    for o in range(15):
        w_copy(o).wait_send()
        f_copy(o).wait_send()

    def s_done(o, c):
        s_copy(o).wait_send()
        return c

    lax.fori_loop(1, KA, s_done, 0)

    def k_done(t, c):
        @pl.when(jnp.logical_not(k_mine(t)))
        def _():
            k_copy(t).wait_send()

        return c

    lax.fori_loop(0, 4, k_done, 0)
    h_copy.wait_send()

    def q_done(t, c):
        @pl.when(red_of(t) != k)
        def _():
            q_copy(t).wait_send()

        return c

    lax.fori_loop(0, 4, q_done, 0)

    @pl.when(is_red)
    def _():
        def o_done(o, c):
            o_copy(o).wait_send()
            return c

        lax.fori_loop(1, KA, o_done, 0)


def hand_over(out_a, sgrad_a, pgrad_a, out_b, sgrad_b, pgrad_b, out_v, sgrad_v, pgrad_v, in_sem, out_sem):
    parts = [
        (pgrad_a.at[pl.ds(n * 8, 8)], pgrad_v.at[pl.ds(n * 8, 8)], pgrad_b.at[pl.ds(n * 8, 8)]) for n in range(8)
    ]
    parts = [(out_a, out_v, out_b), (sgrad_a, sgrad_v, sgrad_b)] + parts
    for n, (src, mid, _) in enumerate(parts):
        pltpu.make_async_copy(src, mid, in_sem.at[n]).start()
    for n, (src, mid, dst) in enumerate(parts):
        pltpu.make_async_copy(src, mid, in_sem.at[n]).wait()
        pltpu.make_async_copy(mid, dst, out_sem.at[n]).start()
    for n, (_, mid, dst) in enumerate(parts):
        pltpu.make_async_copy(mid, dst, out_sem.at[n]).wait()


def local(*args):
    args = args[:10] + (args[10].T,)
    vmem = pl.BlockSpec(memory_space=pltpu.VMEM)
    hbm = pl.BlockSpec(memory_space=pltpu.HBM)
    dma = pltpu.SemaphoreType.DMA
    big = (ROWS, COLS, CP)
    flat = (HEADS * ROWS, 128)
    results = pl.pallas_call(
        kernel,
        out_shape=(
            jax.ShapeDtypeStruct((ROWS, D), BF16),
            jax.ShapeDtypeStruct((ROWS, D), BF16),
            jax.ShapeDtypeStruct(big, BF16),
        ),
        in_specs=[hbm] * 11,
        out_specs=(vmem, vmem, hbm),
        scratch_shapes=[
            pltpu.VMEM(big, BF16),
            pltpu.VMEM((ROWS, D), BF16),
            pltpu.VMEM((COLS,), jnp.int32),
            pltpu.VMEM((ROWS, D), BF16),
            pltpu.VMEM((D,), BF16),
            pltpu.VMEM((HEADS, CP), BF16),
            pltpu.VMEM(big, BF16),
            pltpu.VMEM(big, F32),
            pltpu.VMEM(big, F32),
            pltpu.VMEM(flat, F32),
            pltpu.VMEM(flat, F32),
            pltpu.VMEM((4, 16, D), BF16),
            pltpu.VMEM((ROWS, D), F32),
            pltpu.VMEM((ROWS, 128), F32),
            pltpu.VMEM((2, 4, 16, D), BF16),
            pltpu.VMEM((16, 24, 128), BF16),
            pltpu.VMEM((KA, 16, 24, 128), BF16),
            pltpu.VMEM((16, D, 128), BF16),
            pltpu.VMEM((HEADS * ROWS, D), BF16),
            pltpu.VMEM((HEADS * ROWS, D), BF16),
            pltpu.VMEM((ROWS, D), F32),
            pltpu.VMEM((ROWS, D), F32),
            pltpu.VMEM(flat, F32),
            pltpu.VMEM(flat, F32),
            pltpu.VMEM(flat, BF16),
            pltpu.VMEM(flat, BF16),
            pltpu.VMEM((KA, 24, 128), F32),
            pltpu.VMEM((24, 128), F32),
            pltpu.VMEM((2, ROWS, D), F32),
            pltpu.VMEM((ROWS, D), F32),
            pltpu.VMEM((4, 16, D), BF16),
            pltpu.VMEM((PB // 2, 16, D), BF16),
            pltpu.VMEM((4, 32, D), BF16),
            pltpu.VMEM((KA, 32, D), BF16),
            pltpu.VMEM((32, D), BF16),
            pltpu.VMEM((4, 32, D), BF16),
            dma((4,)), dma((4,)), dma((5,)), dma((16,)),
            dma((4,)), dma, dma, dma,
            dma((15,)), dma((15,)),
            dma((15,)), dma((15,)),
            dma((16,)), dma,
            dma, dma,
            dma((4,)), dma,
            dma((4,)), dma,
            dma((16,)), dma,
        ],
        compiler_params=pltpu.CompilerParams(
            collective_id=0, has_side_effects=True, vmem_limit_bytes=60 * 1024 * 1024),
    )(*args)
    return pl.pallas_call(
        hand_over,
        out_shape=tuple(jax.ShapeDtypeStruct(r.shape, r.dtype) for r in results),
        in_specs=[hbm] * 3,
        out_specs=(hbm,) * 3,
        scratch_shapes=[pltpu.VMEM(r.shape, r.dtype) for r in results] + [dma((10,)), dma((10,))],
        compiler_params=pltpu.CompilerParams(vmem_limit_bytes=60 * 1024 * 1024),
    )(*results)


def solution(mesh):
    in_specs = (
        P("pb", None), P("pb", "ka", None), P("ka"), P("pb", None), P("ka", None), P(),
        P("ka", None), P("ka", None), P("ka", None), P("ka", None), P(),
    )
    out_specs = (P("pb", None), P("pb", None), P("pb", "ka", None))
    return jax.shard_map(local, mesh=mesh, in_specs=in_specs, out_specs=out_specs, check_vma=False)
```

time: 93 us -> 65.3 us (0.70)
  the two profiles are of different devices: /device:TPU:1 before, /device:TPU:8 now
where the time goes in v2:
time: 65.3 us; the launch traced here: 65.1 us
  Pallas kernels  64.5 us (99%)
    pallas_call x1, Pallas kernels, local(): pl.pallas_call(kernel, out_shape=(jax.ShapeDtypeStruct((ROWS, D), BF16),...  62 us
    pallas_call x1, Pallas kernels, local(): pl.pallas_call(hand_over, out_shape=tuple((jax.ShapeDtypeStruct(r.shape,...  2.49 us

profile of v2, /device:TPU:8, one launch (start us, length us, event | category | flops | bytes accessed | tf_op | source)
XLA Modules:
  0.0 65.1 jit_solution(7217022904689558785)
XLA Ops:
  0.6 62.0 %shard_map.130 = (bf16[64,384]{1,0:T(8,128)(2,1)}, bf16[64,384]{1,0:T(8,128)(2,1)}, bf16[64,128,128]{2,1,0:T(8,128)(2,1)}) custom-call(bf16[64,384]{1,0:T(8,128)(2,1)} %single_hbm.1, bf16[64,128,128]{2,1,0:T(8,128)(2,1)} %pair_hbm.1, s32[128]{0:T(128)} %mask_hbm.1, bf16[64,384]{1,0:T(8,128)(2,1)} %ocot_hbm.1, bf16[24,384]{1,0:T(8,128)(2,1)} %wq_hbm.1, ...), custom_call_target="tpu_custom_call" | custom-call | tf_op jit(solution)/shard_map/pallas_call | solution.py:521
  62.6 2.5 %shard_map.131 = (bf16[64,384]{1,0:T(8,128)(2,1)}, bf16[64,384]{1,0:T(8,128)(2,1)}, bf16[64,128,128]{2,1,0:T(8,128)(2,1)}) custom-call(bf16[64,384]{1,0:T(8,128)(2,1)} %get-tuple-element.6.out_a, bf16[64,384]{1,0:T(8,128)(2,1)} %get-tuple-element.7.sgrad_a, bf16[64,128,128]{2,1,0:T(8,128)(2,1)} %get-tuple-element.8.pgrad_a), custom_call_target="tpu_custom_call" | custom-call | tf_op jit(solution)/shard_map/pallas_call | solution.py:580

commit v3 on v2

--- a/solution.py
+++ b/solution.py
@@ -46,10 +46,10 @@
 
 def kernel(
     single_hbm, pair_hbm, mask_hbm, ocot_hbm, wq_hbm, qb_hbm, wk_hbm, wv_hbm, wg_hbm, wo_hbm, pw_hbm,
-    out_ref, sgrad_ref, pgrad_hbm,
+    out_hbm, sgrad_hbm, pgrad_hbm,
     outb,    single_ref, mask_ref, ocot_ref, qb_ref, pw_ref, xp, nrm, invb, bias, sgp, a_i, nsg, isg, xall, wsend, wall, wfull, qbig, gbig, gate_s, cot_s,
-    ebuf, dpbuf, sgb, pbb, stats, stat_send, kv_half, kv_other, kg_send, kg_recv, qg_send, qg_recv, fin_send, fin_recv,
-    in_sem, out_sem, small_sem, wl_sem, x_ss, x_rs, xf_ss, xf_rs, w_ss, w_rs, f_ss, f_rs, s_ss, s_rs, h_ss, h_rs, k_ss, k_rs, q_ss, q_rs, o_ss, o_rs,
+    ebuf, dpbuf, sgb, pbb, stats, stat_send, kv_half, kv_other, kg_send, kg_recv, qg_send, qg_recv, fin_send,
+    in_sem, out_sem, small_sem, wl_sem, x_ss, x_rs, xf_ss, xf_rs, w_ss, w_rs, f_ss, f_rs, s_ss, s_rs, h_ss, h_rs, k_ss, k_rs, q_ss, q_rs, a_ss, a_rs, o_ss, o_rs,
 ):
     p = lax.axis_index("pb")
     k = lax.axis_index("ka")
@@ -72,13 +72,36 @@
         return (p, lax.rem(k + o, KA))
 
     def x_target(o):
-        return (quarter * 8 + lax.rem(p + 2 * o, 8), own)
+        return (lax.rem(chip + o, 16) * 2 + core, own)
 
     def x_source(o):
-        return (2 * k + core, lax.div(p, 8) * 4 + o)
+        return (2 * k + core, quarter * 4 + o)
 
     def pair_in(n):
         return pltpu.make_async_copy(pair_hbm.at[pl.ds(n * 16, 16)], xp.at[pl.ds(n * 16, 16)], in_sem.at[n])
+
+
+    bar = pltpu.get_barrier_semaphore()
+
+    def greet_x(o, c):
+        src = x_source(o)
+
+        @pl.when(jnp.logical_or(src[0] != p, src[1] != k))
+        def _():
+            pl.semaphore_signal(bar, inc=1, device_id=src, device_id_type=MESH)
+
+        return c
+
+    lax.fori_loop(0, 4, greet_x, 0)
+
+    def greet_ka(o, c):
+        pl.semaphore_signal(bar, inc=1, device_id=ka_peer(o), device_id_type=MESH)
+        return c
+
+    lax.fori_loop(1, KA, greet_ka, 0)
+    for a, b in NEAR:
+        pl.semaphore_signal(bar, inc=1, device_id=at(x - a, z - b), device_id_type=MESH)
+    pl.semaphore_signal(bar, inc=1, device_id=sib, device_id_type=MESH)
 
     single_in = pltpu.make_async_copy(single_hbm, single_ref, small_sem.at[0])
     single_in.start()
@@ -97,29 +120,6 @@
         copy.start()
     for n in range(4):
         pair_in(n).start()
-
-    bar = pltpu.get_barrier_semaphore()
-    for a, b in NEAR:
-        pl.semaphore_signal(bar, inc=1, device_id=at(x - a, z - b), device_id_type=MESH)
-
-    def greet_ka(o, c):
-        pl.semaphore_signal(bar, inc=1, device_id=ka_peer(o), device_id_type=MESH)
-        return c
-
-    lax.fori_loop(1, KA, greet_ka, 0)
-    pl.semaphore_signal(bar, inc=1, device_id=sib, device_id_type=MESH)
-
-    def greet_x(o, c):
-        src = x_source(o)
-
-        @pl.when(jnp.logical_or(src[0] != p, src[1] != k))
-        def _():
-            pl.semaphore_signal(bar, inc=1, device_id=src, device_id_type=MESH)
-
-        return c
-
-    lax.fori_loop(0, 4, greet_x, 0)
-
     single_in.wait()
     sv = single_ref[...].astype(F32)
     cen = sv - jnp.mean(sv, axis=-1, keepdims=True)
@@ -135,7 +135,8 @@
     wall[k] = wsend[...]
 
     self_x = own == k
-    pl.semaphore_wait(bar, 15 + 15 + 1 + 4 - self_x.astype(jnp.int32))
+    x_sends = lax.div(own, 4) == quarter
+    pl.semaphore_wait(bar, 15 + 15 + 1 + 16 * x_sends.astype(jnp.int32) - self_x.astype(jnp.int32))
 
     def x_copy(o):
         return pltpu.make_async_remote_copy(
@@ -149,15 +150,17 @@
     def _():
         x_self().start()
 
-    @pl.when(jnp.logical_not(self_x))
+    @pl.when(jnp.logical_and(x_sends, jnp.logical_not(self_x)))
     def _():
         x_copy(0).start()
 
-    def x_send(o, c):
-        x_copy(o).start()
-        return c
-
-    lax.fori_loop(1, 4, x_send, 0)
+    @pl.when(x_sends)
+    def _():
+        def x_send(o, c):
+            x_copy(o).start()
+            return c
+
+        lax.fori_loop(1, 16, x_send, 0)
 
     half = pl.ds(core * 8, 8)
 
@@ -410,64 +413,77 @@
         lax.fori_loop(n * 16, (n + 1) * 16, grad_body, 0, unroll=4)
         pair_out(n).start()
 
+    x_fwd.wait_send()
+
+    @pl.when(jnp.logical_and(x_sends, jnp.logical_not(self_x)))
+    def _():
+        x_copy(0).wait_send()
+
+    @pl.when(x_sends)
+    def _():
+        def x_done(o, c):
+            x_copy(o).wait_send()
+            return c
+
+        lax.fori_loop(1, 16, x_done, 0)
+
+    for o in range(15):
+        w_copy(o).wait_send()
+        f_copy(o).wait_send()
+
+    def s_done(o, c):
+        s_copy(o).wait_send()
+        return c
+
+    lax.fori_loop(1, KA, s_done, 0)
+
     is_red = lax.rem(k, 4) == 1 + core
     t_me = quarter
 
+    r16 = pl.ds(pl.multiple_of(t_me * 16, 16), 16)
+
+    def a_copy(o):
+        return pltpu.make_async_remote_copy(
+            src_ref=fin_send.at[0], dst_ref=out_hbm.at[r16], send_sem=a_ss.at[o], recv_sem=a_rs,
+            device_id=ka_peer(o), device_id_type=MESH)
+
     def o_copy(o):
         return pltpu.make_async_remote_copy(
-            src_ref=fin_send, dst_ref=fin_recv.at[t_me], send_sem=o_ss.at[o], recv_sem=o_rs,
+            src_ref=fin_send.at[1], dst_ref=sgrad_hbm.at[r16], send_sem=o_ss.at[o], recv_sem=o_rs,
             device_id=ka_peer(o), device_id_type=MESH)
 
     @pl.when(is_red)
     def _():
         pltpu.make_async_copy(qg_recv, qg_recv, q_rs).wait()
-        r16 = pl.ds(pl.multiple_of(t_me * 16, 16), 16)
         qa = jnp.sum(qg_recv[...].astype(F32), axis=0)
         g16 = gate_s[r16, :]
         att16 = qa[16:32]
+        fin_send[0] = nn((g16 * att16).astype(BF16), weight(O_T)).astype(BF16)
+
+        def a_start(o, c):
+            a_copy(o).start()
+            return c
+
+        lax.fori_loop(1, KA, a_start, 0)
+        pltpu.make_async_copy(fin_send.at[0], out_hbm.at[r16], a_rs).start()
         gig = cot_s[r16, :] * att16 * g16 * (1.0 - g16)
         part = qa[0:16] + back(gig, G_T)
-        fin_send[16:32, :] = nn((g16 * att16).astype(BF16), weight(O_T)).astype(BF16)
         pltpu.make_async_copy(kg_recv, kg_recv, k_rs).wait()
         ig = part + jnp.sum(kg_recv[...].astype(F32), axis=0)
         n16 = nsg[r16, :]
         sgr = isg[r16, 0:1] * (
             ig - jnp.mean(ig, axis=-1, keepdims=True) - n16 * jnp.mean(ig * n16, axis=-1, keepdims=True))
-        fin_send[0:16, :] = sgr.astype(BF16)
+        fin_send[1] = sgr.astype(BF16)
 
         def o_start(o, c):
             o_copy(o).start()
             return c
 
         lax.fori_loop(1, KA, o_start, 0)
-        pltpu.make_async_copy(fin_send, fin_recv.at[t_me], o_rs).start()
-
-    pltpu.make_async_copy(fin_recv, fin_recv, o_rs).wait()
-    for t in range(4):
-        sgrad_ref[t * 16 : t * 16 + 16, :] = fin_recv[t, 0:16, :]
-        out_ref[t * 16 : t * 16 + 16, :] = fin_recv[t, 16:32, :]
+        pltpu.make_async_copy(fin_send.at[1], sgrad_hbm.at[r16], o_rs).start()
 
     for n in range(4):
         pair_out(n).wait()
-    x_fwd.wait_send()
-    @pl.when(jnp.logical_not(self_x))
-    def _():
-        x_copy(0).wait_send()
-
-    def x_done(o, c):
-        x_copy(o).wait_send()
-        return c
-
-    lax.fori_loop(1, 4, x_done, 0)
-    for o in range(15):
-        w_copy(o).wait_send()
-        f_copy(o).wait_send()
-
-    def s_done(o, c):
-        s_copy(o).wait_send()
-        return c
-
-    lax.fori_loop(1, KA, s_done, 0)
 
     def k_done(t, c):
         @pl.when(jnp.logical_not(k_mine(t)))
@@ -491,10 +507,14 @@
     @pl.when(is_red)
     def _():
         def o_done(o, c):
+            a_copy(o).wait_send()
             o_copy(o).wait_send()
             return c
 
         lax.fori_loop(1, KA, o_done, 0)
+
+    pltpu.make_async_copy(out_hbm, out_hbm, a_rs).wait()
+    pltpu.make_async_copy(sgrad_hbm, sgrad_hbm, o_rs).wait()
 
 
 def hand_over(out_a, sgrad_a, pgrad_a, out_b, sgrad_b, pgrad_b, out_v, sgrad_v, pgrad_v, in_sem, out_sem):
@@ -513,7 +533,6 @@
 
 def local(*args):
     args = args[:10] + (args[10].T,)
-    vmem = pl.BlockSpec(memory_space=pltpu.VMEM)
     hbm = pl.BlockSpec(memory_space=pltpu.HBM)
     dma = pltpu.SemaphoreType.DMA
     big = (ROWS, COLS, CP)
@@ -526,7 +545,7 @@
             jax.ShapeDtypeStruct(big, BF16),
         ),
         in_specs=[hbm] * 11,
-        out_specs=(vmem, vmem, hbm),
+        out_specs=(hbm, hbm, hbm),
         scratch_shapes=[
             pltpu.VMEM(big, BF16),
             pltpu.VMEM((ROWS, D), BF16),
@@ -562,16 +581,16 @@
             pltpu.VMEM((PB // 2, 16, D), BF16),
             pltpu.VMEM((4, 32, D), BF16),
             pltpu.VMEM((KA, 32, D), BF16),
-            pltpu.VMEM((32, D), BF16),
-            pltpu.VMEM((4, 32, D), BF16),
+            pltpu.VMEM((2, 16, D), BF16),
             dma((4,)), dma((4,)), dma((5,)), dma((16,)),
-            dma((4,)), dma, dma, dma,
+            dma((16,)), dma, dma, dma,
             dma((15,)), dma((15,)),
             dma((15,)), dma((15,)),
             dma((16,)), dma,
             dma, dma,
             dma((4,)), dma,
             dma((4,)), dma,
+            dma((16,)), dma,
             dma((16,)), dma,
         ],
         compiler_params=pltpu.CompilerParams(

time: 65.3 us -> 62.9 us (0.963)
  the two profiles are of different devices: /device:TPU:8 before, /device:TPU:56 now
where the time goes in v3:
time: 62.9 us; the launch traced here: 62.8 us
  Pallas kernels  62.1 us (99%)
  between operations  0.64 us (1%)
    pallas_call x1, Pallas kernels, local(): pl.pallas_call(kernel, out_shape=(jax.ShapeDtypeStruct((ROWS, D), BF16),...  59.6 us
    pallas_call x1, Pallas kernels, local(): pl.pallas_call(hand_over, out_shape=tuple((jax.ShapeDtypeStruct(r.shape,...  2.49 us

profile of v3, /device:TPU:56, one launch (start us, length us, event | category | flops | bytes accessed | tf_op | source)
XLA Modules:
  0.0 62.8 jit_solution(14649742746918334180)
XLA Ops:
  0.6 59.6 %shard_map.130 = (bf16[64,384]{1,0:T(8,128)(2,1)}, bf16[64,384]{1,0:T(8,128)(2,1)}, bf16[64,128,128]{2,1,0:T(8,128)(2,1)}) custom-call(bf16[64,384]{1,0:T(8,128)(2,1)} %single_hbm.1, bf16[64,128,128]{2,1,0:T(8,128)(2,1)} %pair_hbm.1, s32[128]{0:T(128)} %mask_hbm.1, bf16[64,384]{1,0:T(8,128)(2,1)} %ocot_hbm.1, bf16[24,384]{1,0:T(8,128)(2,1)} %wq_hbm.1, ...), custom_call_target="tpu_custom_call" | custom-call | tf_op jit(solution)/shard_map/pallas_call | solution.py:540
  60.3 2.5 %shard_map.131 = (bf16[64,384]{1,0:T(8,128)(2,1)}, bf16[64,384]{1,0:T(8,128)(2,1)}, bf16[64,128,128]{2,1,0:T(8,128)(2,1)}) custom-call(bf16[64,384]{1,0:T(8,128)(2,1)} %get-tuple-element.6.out_a, bf16[64,384]{1,0:T(8,128)(2,1)} %get-tuple-element.7.sgrad_a, bf16[64,128,128]{2,1,0:T(8,128)(2,1)} %get-tuple-element.8.pgrad_a), custom_call_target="tpu_custom_call" | custom-call | tf_op jit(solution)/shard_map/pallas_call | solution.py:599

commit v4 on v3

--- a/solution.py
+++ b/solution.py
@@ -47,9 +47,9 @@
 def kernel(
     single_hbm, pair_hbm, mask_hbm, ocot_hbm, wq_hbm, qb_hbm, wk_hbm, wv_hbm, wg_hbm, wo_hbm, pw_hbm,
     out_hbm, sgrad_hbm, pgrad_hbm,
-    outb,    single_ref, mask_ref, ocot_ref, qb_ref, pw_ref, xp, nrm, invb, bias, sgp, a_i, nsg, isg, xall, wsend, wall, wfull, qbig, gbig, gate_s, cot_s,
-    ebuf, dpbuf, sgb, pbb, stats, stat_send, kv_half, kv_other, kg_send, kg_recv, qg_send, qg_recv, fin_send,
-    in_sem, out_sem, small_sem, wl_sem, x_ss, x_rs, xf_ss, xf_rs, w_ss, w_rs, f_ss, f_rs, s_ss, s_rs, h_ss, h_rs, k_ss, k_rs, q_ss, q_rs, a_ss, a_rs, o_ss, o_rs,
+    outb,    single_ref, mask_ref, ocot_ref, qb_ref, pw_ref, xp, nrm, invb, bias, sgp, a_i, nsg, isg, xall, wsend, wall, wfull, qbig, gbig, gate_s, cot_s, cot_send, cot_recv,
+    ebuf, dpbuf, sgb, pbb, stats, stat_send, kv_half, kv_other, kg_send, kg_recv, att_send, att_recv, qg_send, qg_recv, fin_send,
+    in_sem, out_sem, small_sem, wl_sem, x_ss, x_rs, xf_ss, xf_rs, c_ss, c_rs, w_ss, w_rs, f_ss, f_rs, w2_ss, w2_rs, f2_ss, f2_rs, s_ss, s_rs, h_ss, h_rs, k_ss, k_rs, t_ss, t_rs, q_ss, q_rs, a_ss, a_rs, o_ss, o_rs,
 ):
     p = lax.axis_index("pb")
     k = lax.axis_index("ka")
@@ -133,6 +133,11 @@
         copy.wait()
     wsend[15] = jnp.zeros((24, 128), BF16)
     wall[k] = wsend[...]
+    for copy in small_in:
+        copy.wait()
+    own_out = jnp.concatenate([wsend[t] for t in O_T], axis=1)
+    cot_t = nt(own_out, ocot_ref[...])
+    cot_send[...] = jnp.concatenate([cot_t, jnp.zeros((DIM, 128 - ROWS), F32)], axis=1).astype(BF16)
 
     self_x = own == k
     x_sends = lax.div(own, 4) == quarter
@@ -162,7 +167,8 @@
 
         lax.fori_loop(1, 16, x_send, 0)
 
-    half = pl.ds(core * 8, 8)
+    half = pl.ds(core * 8, 6)
+    rest = pl.ds(core * 8 + 6, 2)
 
     def w_copy(o):
         a, b = NEAR[o]
@@ -170,11 +176,28 @@
             src_ref=wsend.at[half], dst_ref=wall.at[k, half], send_sem=w_ss.at[o], recv_sem=w_rs.at[o],
             device_id=at(x + a, z + b), device_id_type=MESH)
 
+    def w2_copy(o):
+        a, b = NEAR[o]
+        return pltpu.make_async_remote_copy(
+            src_ref=wsend.at[rest], dst_ref=wall.at[k, rest], send_sem=w2_ss.at[o], recv_sem=w2_rs.at[o],
+            device_id=at(x + a, z + b), device_id_type=MESH)
+
+    def c_copy(o):
+        return pltpu.make_async_remote_copy(
+            src_ref=cot_send, dst_ref=cot_recv.at[k], send_sem=c_ss.at[o], recv_sem=c_rs,
+            device_id=ka_peer(o), device_id_type=MESH)
+
+    def c_start(o, c):
+        c_copy(o).start()
+        return c
+
+    lax.fori_loop(1, KA, c_start, 0)
+    pltpu.make_async_copy(cot_send, cot_recv.at[k], c_rs).start()
     for o in range(15):
         w_copy(o).start()
-
-    for copy in small_in:
-        copy.wait()
+    for o in range(15):
+        w2_copy(o).start()
+
     pwt_b = pw_ref[...]
     pwt = pwt_b.astype(F32)
 
@@ -207,6 +230,13 @@
             src_ref=wall.at[src, half], dst_ref=wall.at[src, half], send_sem=f_ss.at[o], recv_sem=f_rs.at[o],
             device_id=sib, device_id_type=MESH)
 
+    def f2_copy(o):
+        a, b = NEAR[o]
+        src = at(x - a, z - b)[1]
+        return pltpu.make_async_remote_copy(
+            src_ref=wall.at[src, rest], dst_ref=wall.at[src, rest], send_sem=f2_ss.at[o], recv_sem=f2_rs.at[o],
+            device_id=sib, device_id_type=MESH)
+
     for o in range(15):
         w_copy(o).wait_recv()
         f_copy(o).start()
@@ -217,14 +247,14 @@
         device_id=sib, device_id_type=MESH)
     x_fwd.start()
 
-    def build(first):
-        for n in range(8):
+    def build(first, count):
+        for n in range(count):
             wfull[first + n] = wall[:, first + n].astype(F32).reshape(D, 128).astype(BF16)
 
-    build(core * 8)
+    build(core * 8, 6)
     for o in range(15):
         f_copy(o).wait_recv()
-    build(8 - core * 8)
+    build(8 - core * 8, 6)
     x_fwd.wait_recv()
 
     def weight(tiles):
@@ -236,7 +266,8 @@
     values = nn(keys_in, weight(V_T)).astype(BF16)
     queries = (nn(rows_in, weight(Q_T)) + qb_ref[...].astype(F32).reshape(1, D)).astype(BF16)
     gate = jax.nn.sigmoid(nn(rows_in, weight(G_T)))
-    cot = nt(ocot_ref[...], weight(O_T))
+    pltpu.make_async_copy(cot_recv, cot_recv, c_rs).wait()
+    cot = cot_recv[...].astype(F32).reshape(D, 128).T[0:ROWS]
     gate_s[...] = gate
     cot_s[...] = cot
     agrad = (gate * cot).astype(BF16)
@@ -284,6 +315,9 @@
 
     lax.fori_loop(1, KA, s_start, 0)
     pltpu.make_async_copy(stat_send, stats.at[k], s_rs).start()
+    for o in range(15):
+        w2_copy(o).wait_recv()
+        f2_copy(o).start()
     num = jnp.zeros((ROWS, D), F32)
     for h in range(HEADS):
         rows = slice(h * ROWS, (h + 1) * ROWS)
@@ -299,19 +333,43 @@
     coef = jnp.exp(pm - gm) / gt
     delta = gd / gt
     coef_f = jnp.zeros((ROWS, D), F32)
+    for h in range(HEADS):
+        cc = jnp.concatenate([jnp.broadcast_to(coef[:, g * 16 + h : g * 16 + h + 1], (8, 128)) for g in range(8)], axis=0)
+        coef_f = coef_f + jnp.concatenate([cc] * 3, axis=1) * heads_f[h]
+    att_send[...] = (num * coef_f).astype(BF16).reshape(4, 16, D)
+
+    def red_of(t):
+        return 4 * t + 1 + core
+
+    def t_copy(t):
+        return pltpu.make_async_remote_copy(
+            src_ref=att_send.at[t], dst_ref=att_recv.at[k], send_sem=t_ss.at[t], recv_sem=t_rs,
+            device_id=(p, red_of(t)), device_id_type=MESH)
+
+    def t_start(t, c):
+        mine = red_of(t) == k
+
+        @pl.when(mine)
+        def _():
+            pltpu.make_async_copy(att_send.at[t], att_recv.at[k], t_rs).start()
+
+        @pl.when(jnp.logical_not(mine))
+        def _():
+            t_copy(t).start()
+
+        return c
+
+    lax.fori_loop(0, 4, t_start, 0)
 
     for h in range(HEADS):
         rows = slice(h * ROWS, (h + 1) * ROWS)
         cc = jnp.concatenate([jnp.broadcast_to(coef[:, g * 16 + h : g * 16 + h + 1], (8, 128)) for g in range(8)], axis=0)
         dc = jnp.concatenate([jnp.broadcast_to(delta[:, g * 16 + h : g * 16 + h + 1], (8, 128)) for g in range(8)], axis=0)
-        coef_f = coef_f + jnp.concatenate([cc] * 3, axis=1) * heads_f[h]
         prob = ebuf[rows, :] * cc
         sg = prob * (dpbuf[rows, :] - dc)
         sgp[pl.ds(h, ROWS, stride=HEADS), :] = sg
         sgb[rows, :] = sg.astype(BF16)
         pbb[rows, :] = prob.astype(BF16)
-
-    att = num * coef_f
 
     def back(v, n):
         hi, lo = split2(v)
@@ -331,15 +389,31 @@
         rows = slice(h * ROWS, (h + 1) * ROWS)
         qg = qg + nn(sgb[rows, :], keys) * heads_f[h]
     row_in = back(qg * SCALE, Q_T)
-    for t in range(4):
-        qg_send[t, 0:16, :] = row_in[t * 16 : t * 16 + 16].astype(BF16)
+    qg_send[...] = row_in.astype(BF16).reshape(4, 16, D)
+
+    def q_copy(t):
+        return pltpu.make_async_remote_copy(
+            src_ref=qg_send.at[t], dst_ref=qg_recv.at[k], send_sem=q_ss.at[t], recv_sem=q_rs,
+            device_id=(p, red_of(t)), device_id_type=MESH)
+
+    def q_start(t, c):
+        mine = red_of(t) == k
+
+        @pl.when(mine)
+        def _():
+            pltpu.make_async_copy(qg_send.at[t], qg_recv.at[k], q_rs).start()
+
+        @pl.when(jnp.logical_not(mine))
+        def _():
+            q_copy(t).start()
+
+        return c
+
+    lax.fori_loop(0, 4, q_start, 0)
 
     h_copy.wait_recv()
     kg_send[...] = (kv_half[core] + kv_other[...]).astype(BF16).reshape(4, 16, D)
 
-    def red_of(t):
-        return 4 * t + 1 + core
-
     def k_copy(t):
         return pltpu.make_async_remote_copy(
             src_ref=kg_send.at[t], dst_ref=kg_recv.at[chip], send_sem=k_ss.at[t], recv_sem=k_rs,
@@ -362,29 +436,6 @@
         return c
 
     lax.fori_loop(0, 4, k_start, 0)
-
-    for t in range(4):
-        qg_send[t, 16:32, :] = att[t * 16 : t * 16 + 16].astype(BF16)
-
-    def q_copy(t):
-        return pltpu.make_async_remote_copy(
-            src_ref=qg_send.at[t], dst_ref=qg_recv.at[k], send_sem=q_ss.at[t], recv_sem=q_rs,
-            device_id=(p, red_of(t)), device_id_type=MESH)
-
-    def q_start(t, c):
-        mine = red_of(t) == k
-
-        @pl.when(mine)
-        def _():
-            pltpu.make_async_copy(qg_send.at[t], qg_recv.at[k], q_rs).start()
-
-        @pl.when(jnp.logical_not(mine))
-        def _():
-            q_copy(t).start()
-
-        return c
-
-    lax.fori_loop(0, 4, q_start, 0)
 
     wc = pwt - jnp.mean(pwt, axis=-1, keepdims=True)
     wc_hi, wc_lo = split2(wc)
@@ -413,6 +464,11 @@
         lax.fori_loop(n * 16, (n + 1) * 16, grad_body, 0, unroll=4)
         pair_out(n).start()
 
+    for o in range(15):
+        f2_copy(o).wait_recv()
+    build(6, 2)
+    build(14, 2)
+
     x_fwd.wait_send()
 
     @pl.when(jnp.logical_and(x_sends, jnp.logical_not(self_x)))
@@ -430,9 +486,12 @@
     for o in range(15):
         w_copy(o).wait_send()
         f_copy(o).wait_send()
+        w2_copy(o).wait_send()
+        f2_copy(o).wait_send()
 
     def s_done(o, c):
         s_copy(o).wait_send()
+        c_copy(o).wait_send()
         return c
 
     lax.fori_loop(1, KA, s_done, 0)
@@ -454,10 +513,9 @@
 
     @pl.when(is_red)
     def _():
-        pltpu.make_async_copy(qg_recv, qg_recv, q_rs).wait()
-        qa = jnp.sum(qg_recv[...].astype(F32), axis=0)
+        pltpu.make_async_copy(att_recv, att_recv, t_rs).wait()
+        att16 = jnp.sum(att_recv[...].astype(F32), axis=0)
         g16 = gate_s[r16, :]
-        att16 = qa[16:32]
         fin_send[0] = nn((g16 * att16).astype(BF16), weight(O_T)).astype(BF16)
 
         def a_start(o, c):
@@ -467,7 +525,9 @@
         lax.fori_loop(1, KA, a_start, 0)
         pltpu.make_async_copy(fin_send.at[0], out_hbm.at[r16], a_rs).start()
         gig = cot_s[r16, :] * att16 * g16 * (1.0 - g16)
-        part = qa[0:16] + back(gig, G_T)
+        part = back(gig, G_T)
+        pltpu.make_async_copy(qg_recv, qg_recv, q_rs).wait()
+        part = part + jnp.sum(qg_recv[...].astype(F32), axis=0)
         pltpu.make_async_copy(kg_recv, kg_recv, k_rs).wait()
         ig = part + jnp.sum(kg_recv[...].astype(F32), axis=0)
         n16 = nsg[r16, :]
@@ -499,6 +559,7 @@
         @pl.when(red_of(t) != k)
         def _():
             q_copy(t).wait_send()
+            t_copy(t).wait_send()
 
         return c
 
@@ -569,6 +630,8 @@
             pltpu.VMEM((HEADS * ROWS, D), BF16),
             pltpu.VMEM((ROWS, D), F32),
             pltpu.VMEM((ROWS, D), F32),
+            pltpu.VMEM((DIM, 128), BF16),
+            pltpu.VMEM((KA, DIM, 128), BF16),
             pltpu.VMEM(flat, F32),
             pltpu.VMEM(flat, F32),
             pltpu.VMEM(flat, BF16),
@@ -579,15 +642,21 @@
             pltpu.VMEM((ROWS, D), F32),
             pltpu.VMEM((4, 16, D), BF16),
             pltpu.VMEM((PB // 2, 16, D), BF16),
-            pltpu.VMEM((4, 32, D), BF16),
-            pltpu.VMEM((KA, 32, D), BF16),
+            pltpu.VMEM((4, 16, D), BF16),
+            pltpu.VMEM((KA, 16, D), BF16),
+            pltpu.VMEM((4, 16, D), BF16),
+            pltpu.VMEM((KA, 16, D), BF16),
             pltpu.VMEM((2, 16, D), BF16),
             dma((4,)), dma((4,)), dma((5,)), dma((16,)),
             dma((16,)), dma, dma, dma,
+            dma((16,)), dma,
+            dma((15,)), dma((15,)),
+            dma((15,)), dma((15,)),
             dma((15,)), dma((15,)),
             dma((15,)), dma((15,)),
             dma((16,)), dma,
             dma, dma,
+            dma((4,)), dma,
             dma((4,)), dma,
             dma((4,)), dma,
             dma((16,)), dma,

time: 62.9 us -> 62.9 us (level); the launches traced: 62.8 us -> 61.7 us
  Pallas kernels: 62.1 us -> 61.1 us
    pallas_call x1, Pallas kernels: 59.6 us -> 58.6 us  [local(): pl.pallas_call(kernel, out_shape=(jax.ShapeDtypeStruct((ROWS, D), BF16),...]
where the time goes in v4:
time: 62.9 us; the launch traced here: 61.7 us
  Pallas kernels  61.1 us (97%)
  between operations  0.64 us (1%)
    pallas_call x1, Pallas kernels, local(): pl.pallas_call(kernel, out_shape=(jax.ShapeDtypeStruct((ROWS, D), BF16),...  58.6 us
    pallas_call x1, Pallas kernels, local(): pl.pallas_call(hand_over, out_shape=tuple((jax.ShapeDtypeStruct(r.shape,...  2.49 us

profile of v4, /device:TPU:56, one launch (start us, length us, event | category | flops | bytes accessed | tf_op | source)
XLA Modules:
  0.0 61.7 jit_solution(14063672631005356701)
XLA Ops:
  0.6 58.6 %shard_map.130 = (bf16[64,384]{1,0:T(8,128)(2,1)}, bf16[64,384]{1,0:T(8,128)(2,1)}, bf16[64,128,128]{2,1,0:T(8,128)(2,1)}) custom-call(bf16[64,384]{1,0:T(8,128)(2,1)} %single_hbm.1, bf16[64,128,128]{2,1,0:T(8,128)(2,1)} %pair_hbm.1, s32[128]{0:T(128)} %mask_hbm.1, bf16[64,384]{1,0:T(8,128)(2,1)} %ocot_hbm.1, bf16[24,384]{1,0:T(8,128)(2,1)} %wq_hbm.1, ...), custom_call_target="tpu_custom_call" | custom-call | tf_op jit(solution)/shard_map/pallas_call | solution.py:601
  59.2 2.5 %shard_map.131 = (bf16[64,384]{1,0:T(8,128)(2,1)}, bf16[64,384]{1,0:T(8,128)(2,1)}, bf16[64,128,128]{2,1,0:T(8,128)(2,1)}) custom-call(bf16[64,384]{1,0:T(8,128)(2,1)} %get-tuple-element.6.out_a, bf16[64,384]{1,0:T(8,128)(2,1)} %get-tuple-element.7.sgrad_a, bf16[64,128,128]{2,1,0:T(8,128)(2,1)} %get-tuple-element.8.pgrad_a), custom_call_target="tpu_custom_call" | custom-call | tf_op jit(solution)/shard_map/pallas_call | solution.py:668

commit v5 on v4

--- a/solution.py
+++ b/solution.py
@@ -47,9 +47,9 @@
 def kernel(
     single_hbm, pair_hbm, mask_hbm, ocot_hbm, wq_hbm, qb_hbm, wk_hbm, wv_hbm, wg_hbm, wo_hbm, pw_hbm,
     out_hbm, sgrad_hbm, pgrad_hbm,
-    outb,    single_ref, mask_ref, ocot_ref, qb_ref, pw_ref, xp, nrm, invb, bias, sgp, a_i, nsg, isg, xall, wsend, wall, wfull, qbig, gbig, gate_s, cot_s, cot_send, cot_recv,
+    outb,    single_ref, mask_ref, ocot_ref, qb_ref, pw_ref, xp, nrm, invb, bias, sgp, a_i, nsg, isg, xall, wsend, wall, wfull, qbig, gbig, gate_s, cot_s,
     ebuf, dpbuf, sgb, pbb, stats, stat_send, kv_half, kv_other, kg_send, kg_recv, att_send, att_recv, qg_send, qg_recv, fin_send,
-    in_sem, out_sem, small_sem, wl_sem, x_ss, x_rs, xf_ss, xf_rs, c_ss, c_rs, w_ss, w_rs, f_ss, f_rs, w2_ss, w2_rs, f2_ss, f2_rs, s_ss, s_rs, h_ss, h_rs, k_ss, k_rs, t_ss, t_rs, q_ss, q_rs, a_ss, a_rs, o_ss, o_rs,
+    in_sem, out_sem, small_sem, wl_sem, x_ss, x_rs, xf_ss, xf_rs, w_ss, w_rs, f_ss, f_rs, s_ss, s_rs, h_ss, h_rs, k_ss, k_rs, t_ss, t_rs, q_ss, q_rs, a_ss, a_rs, o_ss, o_rs,
 ):
     p = lax.axis_index("pb")
     k = lax.axis_index("ka")
@@ -133,11 +133,6 @@
         copy.wait()
     wsend[15] = jnp.zeros((24, 128), BF16)
     wall[k] = wsend[...]
-    for copy in small_in:
-        copy.wait()
-    own_out = jnp.concatenate([wsend[t] for t in O_T], axis=1)
-    cot_t = nt(own_out, ocot_ref[...])
-    cot_send[...] = jnp.concatenate([cot_t, jnp.zeros((DIM, 128 - ROWS), F32)], axis=1).astype(BF16)
 
     self_x = own == k
     x_sends = lax.div(own, 4) == quarter
@@ -167,8 +162,7 @@
 
         lax.fori_loop(1, 16, x_send, 0)
 
-    half = pl.ds(core * 8, 6)
-    rest = pl.ds(core * 8 + 6, 2)
+    half = pl.ds(core * 8, 8)
 
     def w_copy(o):
         a, b = NEAR[o]
@@ -176,28 +170,11 @@
             src_ref=wsend.at[half], dst_ref=wall.at[k, half], send_sem=w_ss.at[o], recv_sem=w_rs.at[o],
             device_id=at(x + a, z + b), device_id_type=MESH)
 
-    def w2_copy(o):
-        a, b = NEAR[o]
-        return pltpu.make_async_remote_copy(
-            src_ref=wsend.at[rest], dst_ref=wall.at[k, rest], send_sem=w2_ss.at[o], recv_sem=w2_rs.at[o],
-            device_id=at(x + a, z + b), device_id_type=MESH)
-
-    def c_copy(o):
-        return pltpu.make_async_remote_copy(
-            src_ref=cot_send, dst_ref=cot_recv.at[k], send_sem=c_ss.at[o], recv_sem=c_rs,
-            device_id=ka_peer(o), device_id_type=MESH)
-
-    def c_start(o, c):
-        c_copy(o).start()
-        return c
-
-    lax.fori_loop(1, KA, c_start, 0)
-    pltpu.make_async_copy(cot_send, cot_recv.at[k], c_rs).start()
     for o in range(15):
         w_copy(o).start()
-    for o in range(15):
-        w2_copy(o).start()
-
+
+    for copy in small_in:
+        copy.wait()
     pwt_b = pw_ref[...]
     pwt = pwt_b.astype(F32)
 
@@ -230,13 +207,6 @@
             src_ref=wall.at[src, half], dst_ref=wall.at[src, half], send_sem=f_ss.at[o], recv_sem=f_rs.at[o],
             device_id=sib, device_id_type=MESH)
 
-    def f2_copy(o):
-        a, b = NEAR[o]
-        src = at(x - a, z - b)[1]
-        return pltpu.make_async_remote_copy(
-            src_ref=wall.at[src, rest], dst_ref=wall.at[src, rest], send_sem=f2_ss.at[o], recv_sem=f2_rs.at[o],
-            device_id=sib, device_id_type=MESH)
-
     for o in range(15):
         w_copy(o).wait_recv()
         f_copy(o).start()
@@ -247,14 +217,14 @@
         device_id=sib, device_id_type=MESH)
     x_fwd.start()
 
-    def build(first, count):
-        for n in range(count):
+    def build(first):
+        for n in range(8):
             wfull[first + n] = wall[:, first + n].astype(F32).reshape(D, 128).astype(BF16)
 
-    build(core * 8, 6)
+    build(core * 8)
     for o in range(15):
         f_copy(o).wait_recv()
-    build(8 - core * 8, 6)
+    build(8 - core * 8)
     x_fwd.wait_recv()
 
     def weight(tiles):
@@ -266,8 +236,7 @@
     values = nn(keys_in, weight(V_T)).astype(BF16)
     queries = (nn(rows_in, weight(Q_T)) + qb_ref[...].astype(F32).reshape(1, D)).astype(BF16)
     gate = jax.nn.sigmoid(nn(rows_in, weight(G_T)))
-    pltpu.make_async_copy(cot_recv, cot_recv, c_rs).wait()
-    cot = cot_recv[...].astype(F32).reshape(D, 128).T[0:ROWS]
+    cot = nt(ocot_ref[...], weight(O_T))
     gate_s[...] = gate
     cot_s[...] = cot
     agrad = (gate * cot).astype(BF16)
@@ -315,9 +284,6 @@
 
     lax.fori_loop(1, KA, s_start, 0)
     pltpu.make_async_copy(stat_send, stats.at[k], s_rs).start()
-    for o in range(15):
-        w2_copy(o).wait_recv()
-        f2_copy(o).start()
     num = jnp.zeros((ROWS, D), F32)
     for h in range(HEADS):
         rows = slice(h * ROWS, (h + 1) * ROWS)
@@ -376,7 +342,8 @@
         w = weight(n)
         return nt(hi, w) + nt(lo, w)
 
-    key_in = back(tn(sgb[...], qbig[...]) * SCALE, K_T) + back(tn(pbb[...], gbig[...]), V_T)
+    key_in = nt((tn(sgb[...], qbig[...]) * SCALE).astype(BF16), weight(K_T)) + nt(
+        tn(pbb[...], gbig[...]).astype(BF16), weight(V_T))
     kv_half[0] = key_in[0:ROWS]
     kv_half[1] = key_in[ROWS : 2 * ROWS]
     h_copy = pltpu.make_async_remote_copy(
@@ -388,7 +355,7 @@
     for h in range(HEADS):
         rows = slice(h * ROWS, (h + 1) * ROWS)
         qg = qg + nn(sgb[rows, :], keys) * heads_f[h]
-    row_in = back(qg * SCALE, Q_T)
+    row_in = nt((qg * SCALE).astype(BF16), weight(Q_T))
     qg_send[...] = row_in.astype(BF16).reshape(4, 16, D)
 
     def q_copy(t):
@@ -464,11 +431,6 @@
         lax.fori_loop(n * 16, (n + 1) * 16, grad_body, 0, unroll=4)
         pair_out(n).start()
 
-    for o in range(15):
-        f2_copy(o).wait_recv()
-    build(6, 2)
-    build(14, 2)
-
     x_fwd.wait_send()
 
     @pl.when(jnp.logical_and(x_sends, jnp.logical_not(self_x)))
@@ -486,12 +448,9 @@
     for o in range(15):
         w_copy(o).wait_send()
         f_copy(o).wait_send()
-        w2_copy(o).wait_send()
-        f2_copy(o).wait_send()
 
     def s_done(o, c):
         s_copy(o).wait_send()
-        c_copy(o).wait_send()
         return c
 
     lax.fori_loop(1, KA, s_done, 0)
@@ -630,8 +589,6 @@
             pltpu.VMEM((HEADS * ROWS, D), BF16),
             pltpu.VMEM((ROWS, D), F32),
             pltpu.VMEM((ROWS, D), F32),
-            pltpu.VMEM((DIM, 128), BF16),
-            pltpu.VMEM((KA, DIM, 128), BF16),
             pltpu.VMEM(flat, F32),
             pltpu.VMEM(flat, F32),
             pltpu.VMEM(flat, BF16),
@@ -649,9 +606,6 @@
             pltpu.VMEM((2, 16, D), BF16),
             dma((4,)), dma((4,)), dma((5,)), dma((16,)),
             dma((16,)), dma, dma, dma,
-            dma((16,)), dma,
-            dma((15,)), dma((15,)),
-            dma((15,)), dma((15,)),
             dma((15,)), dma((15,)),
             dma((15,)), dma((15,)),
             dma((16,)), dma,

time: 62.9 us -> 61.4 us (0.976)
  Pallas kernels: 61.1 us -> 59.9 us
    pallas_call x1, Pallas kernels: 58.6 us -> 57.4 us  [local(): pl.pallas_call(kernel, out_shape=(jax.ShapeDtypeStruct((ROWS, D), BF16),...]
where the time goes in v5:
time: 61.4 us; the launch traced here: 60.5 us
  Pallas kernels  59.9 us (98%)
  between operations  0.64 us (1%)
    pallas_call x1, Pallas kernels, local(): pl.pallas_call(kernel, out_shape=(jax.ShapeDtypeStruct((ROWS, D), BF16),...  57.4 us
    pallas_call x1, Pallas kernels, local(): pl.pallas_call(hand_over, out_shape=tuple((jax.ShapeDtypeStruct(r.shape,...  2.49 us

profile of v5, /device:TPU:56, one launch (start us, length us, event | category | flops | bytes accessed | tf_op | source)
XLA Modules:
  0.0 60.5 jit_solution(13199101905847411317)
XLA Ops:
  0.6 57.4 %shard_map.130 = (bf16[64,384]{1,0:T(8,128)(2,1)}, bf16[64,384]{1,0:T(8,128)(2,1)}, bf16[64,128,128]{2,1,0:T(8,128)(2,1)}) custom-call(bf16[64,384]{1,0:T(8,128)(2,1)} %single_hbm.1, bf16[64,128,128]{2,1,0:T(8,128)(2,1)} %pair_hbm.1, s32[128]{0:T(128)} %mask_hbm.1, bf16[64,384]{1,0:T(8,128)(2,1)} %ocot_hbm.1, bf16[24,384]{1,0:T(8,128)(2,1)} %wq_hbm.1, ...), custom_call_target="tpu_custom_call" | custom-call | tf_op jit(solution)/shard_map/pallas_call | solution.py:560
  58.0 2.5 %shard_map.131 = (bf16[64,384]{1,0:T(8,128)(2,1)}, bf16[64,384]{1,0:T(8,128)(2,1)}, bf16[64,128,128]{2,1,0:T(8,128)(2,1)}) custom-call(bf16[64,384]{1,0:T(8,128)(2,1)} %get-tuple-element.6.out_a, bf16[64,384]{1,0:T(8,128)(2,1)} %get-tuple-element.7.sgrad_a, bf16[64,128,128]{2,1,0:T(8,128)(2,1)} %get-tuple-element.8.pgrad_a), custom_call_target="tpu_custom_call" | custom-call | tf_op jit(solution)/shard_map/pallas_call | solution.py:622

commit v6 on v5

--- a/solution.py
+++ b/solution.py
@@ -196,18 +196,22 @@
             bias[pl.ds(pl.multiple_of(n * 128 + m * 16, 16), 16), :] = both[:, m * 128 : (m + 1) * 128]
         return c
 
+    def f_copy(o):
+        a, b = NEAR[o]
+        src = at(x - a, z - b)[1]
+        return pltpu.make_async_remote_copy(
+            src_ref=wall.at[src, half], dst_ref=wall.at[src, half], send_sem=f_ss.at[o], recv_sem=f_rs.at[o],
+            device_id=sib, device_id_type=MESH)
+
     for n in range(4):
         pair_in(n).wait()
         lax.fori_loop(n * 2, n * 2 + 2, pair_body, 0)
-
-    def f_copy(o):
-        a, b = NEAR[o]
-        src = at(x - a, z - b)[1]
-        return pltpu.make_async_remote_copy(
-            src_ref=wall.at[src, half], dst_ref=wall.at[src, half], send_sem=f_ss.at[o], recv_sem=f_rs.at[o],
-            device_id=sib, device_id_type=MESH)
-
-    for o in range(15):
+        if n == 2:
+            for o in range(6):
+                w_copy(o).wait_recv()
+                f_copy(o).start()
+
+    for o in range(6, 15):
         w_copy(o).wait_recv()
         f_copy(o).start()
 

time: 61.4 us -> 61.4 us (level)
  no operation moved by 1% of the time
where the time goes in v6:
time: 61.4 us; the launch traced here: 60.5 us
  Pallas kernels  59.9 us (98%)
  between operations  0.64 us (1%)
    pallas_call x1, Pallas kernels, local(): pl.pallas_call(kernel, out_shape=(jax.ShapeDtypeStruct((ROWS, D), BF16),...  57.4 us
    pallas_call x1, Pallas kernels, local(): pl.pallas_call(hand_over, out_shape=tuple((jax.ShapeDtypeStruct(r.shape,...  2.49 us

profile of v6, /device:TPU:56, one launch (start us, length us, event | category | flops | bytes accessed | tf_op | source)
XLA Modules:
  0.0 60.5 jit_solution(9390272641079668113)
XLA Ops:
  0.6 57.4 %shard_map.130 = (bf16[64,384]{1,0:T(8,128)(2,1)}, bf16[64,384]{1,0:T(8,128)(2,1)}, bf16[64,128,128]{2,1,0:T(8,128)(2,1)}) custom-call(bf16[64,384]{1,0:T(8,128)(2,1)} %single_hbm.1, bf16[64,128,128]{2,1,0:T(8,128)(2,1)} %pair_hbm.1, s32[128]{0:T(128)} %mask_hbm.1, bf16[64,384]{1,0:T(8,128)(2,1)} %ocot_hbm.1, bf16[24,384]{1,0:T(8,128)(2,1)} %wq_hbm.1, ...), custom_call_target="tpu_custom_call" | custom-call | tf_op jit(solution)/shard_map/pallas_call | solution.py:564
  58.0 2.5 %shard_map.131 = (bf16[64,384]{1,0:T(8,128)(2,1)}, bf16[64,384]{1,0:T(8,128)(2,1)}, bf16[64,128,128]{2,1,0:T(8,128)(2,1)}) custom-call(bf16[64,384]{1,0:T(8,128)(2,1)} %get-tuple-element.6.out_a, bf16[64,384]{1,0:T(8,128)(2,1)} %get-tuple-element.7.sgrad_a, bf16[64,128,128]{2,1,0:T(8,128)(2,1)} %get-tuple-element.8.pgrad_a), custom_call_target="tpu_custom_call" | custom-call | tf_op jit(solution)/shard_map/pallas_call | solution.py:626
